TPU v7x, 128 devices: a whole 4x4x4 slice. The times are simulated.
128 devices in a mesh: band: 8 (over y, core), tile: 16 (over x, z).
Axes of the slice: x: 4, y: 4, z: 4, core: 2. Of those that a mesh axis runs over, the one named last changes fastest.
Arguments:
- grid_in: bfloat16 [524288, 227], P(('band', 'tile')), may hold values from -6 to 6
- embed_in: bfloat16 [227, 512], replicated, may hold values from -0.375 to 0.375
- embed_out: bfloat16 [512, 512], replicated, may hold values from -0.25 to 0.25
- mesh_latent: bfloat16 [327680, 512], P(('band', 'tile')), may hold values from -6 to 6
- edge_latent: bfloat16 [524288, 512], P(('band', 'tile')), may hold values from -6 to 6
- enc_w: bfloat16 [3, 512, 512], replicated, may hold values from -0.25 to 0.25
- node_w: bfloat16 [3, 512, 512], replicated, may hold values from -0.25 to 0.25
- proc_w: bfloat16 [4, 512, 512], replicated, may hold values from -0.25 to 0.25
- gains: float32 [3, 512], replicated, may hold values from 0.1 to 1.9
- g2m_src: int32 [128, 128, 16], P(('band', 'tile')), may hold values from 0 to 4095
- g2m_dst: int32 [128, 128, 16], P(('band', 'tile')), may hold values from 0 to 2559
- g2m_count: int32 [128, 128], P(('band', 'tile')), may hold values from 0 to 16, as said below
- halo_rows: int32 [128, 128, 16], P(('band', 'tile')), may hold values from 0 to 2559
- proc_dst: int32 [524288], P(('band', 'tile')), may hold values from 0 to 2559
- proc_src: int32 [524288], P(('band', 'tile')), may hold values from 0 to 4607, as said below
Outputs:
- mesh_out: bfloat16 [327680, 512], P(('band', 'tile'))
- edge_out: bfloat16 [524288, 512], P(('band', 'tile'))
Inputs may be any that keep to these rules, and one draw needn't show every extreme that they name: `g2m_count`: every sender has live slots to every receiver, at most 16 from each; some receiver has 16 from each of its senders. `proc_src`: halo slots are read from every device other than the reader itself, and every such slot is read by some edge.
All inputs are finite; a program needn't handle non-finite values.
Results may differ from a plain program's by a relative error of at most 0.007.
Values may be sent and summed in bfloat16 or wider, within the bound.
No kernel may reach another device: no remote copies, remote signals or barrier semaphores. Data moves between devices by JAX's collectives and lax.ppermute only.
A program may use at most 128 MiB of HBM per device.

v0:
```python
import jax
import jax.numpy as jnp
from jax import lax
from jax.sharding import PartitionSpec as P


def layer_norm(value, gain):
    mean = jnp.mean(value, axis=-1, keepdims=True)
    centred = value - mean
    variance = jnp.mean(centred * centred, axis=-1, keepdims=True)
    return centred / jnp.sqrt(variance + 1e-05) * gain


def shards(
    grid_in,
    embed_in,
    embed_out,
    mesh_latent,
    edge_latent,
    enc_w,
    node_w,
    proc_w,
    gains,
    g2m_src,
    g2m_dst,
    g2m_count,
    halo_rows,
    proc_dst,
    proc_src,
):
    n_band = lax.axis_size("band")
    n_tile = lax.axis_size("tile")
    peers = n_band * n_tile
    width = mesh_latent.shape[1]
    slots = g2m_src.shape[2]
    halo_slots = halo_rows.shape[2]
    mesh_rows = mesh_latent.shape[0]
    grid_hidden = jax.nn.silu(
        jnp.dot(grid_in, embed_in, preferred_element_type=jnp.float32)
    ).astype(jnp.bfloat16)
    grid_latent = layer_norm(
        jnp.dot(grid_hidden, embed_out, preferred_element_type=jnp.float32), gains[0]
    ).astype(jnp.bfloat16)
    outgoing = grid_latent[g2m_src[0].reshape(-1)].reshape(peers, slots, width)
    arrived = lax.all_to_all(outgoing, ("band", "tile"), split_axis=0, concat_axis=0, tiled=True)
    received = arrived.reshape(peers * slots, width)
    mesh_proj = jnp.dot(mesh_latent, enc_w[1], preferred_element_type=jnp.float32)
    own_term = jnp.dot(mesh_latent, node_w[0], preferred_element_type=jnp.float32)
    edge_term = jnp.dot(edge_latent, proc_w[0], preferred_element_type=jnp.float32)
    dst_flat = g2m_dst[0].reshape(-1)
    edge_hidden = jax.nn.silu(
        jnp.dot(received, enc_w[0], preferred_element_type=jnp.float32) + mesh_proj[dst_flat]
    ).astype(jnp.bfloat16)
    message = jnp.dot(edge_hidden, enc_w[2], preferred_element_type=jnp.float32)
    live = (jnp.arange(slots, dtype=jnp.int32)[None, :] < g2m_count[0][:, None]).reshape(-1, 1)
    message = jnp.where(live, message, jnp.float32(0.0))
    aggregate = (
        jnp.zeros((mesh_rows, width), jnp.float32).at[dst_flat].add(message).astype(jnp.bfloat16)
    )
    node_hidden = jax.nn.silu(
        own_term + jnp.dot(aggregate, node_w[1], preferred_element_type=jnp.float32)
    ).astype(jnp.bfloat16)
    update = layer_norm(
        jnp.dot(node_hidden, node_w[2], preferred_element_type=jnp.float32), gains[1]
    )
    mesh_new = (mesh_latent.astype(jnp.float32) + update).astype(jnp.bfloat16)
    halo_out = mesh_new[halo_rows[0].reshape(-1)].reshape(peers, halo_slots, width)
    halo_in = lax.all_to_all(halo_out, ("band", "tile"), split_axis=0, concat_axis=0, tiled=True)
    table = jnp.concatenate([mesh_new, halo_in.reshape(peers * halo_slots, width)], axis=0)
    receiver = mesh_new[proc_dst]
    sender = table[proc_src]
    pre = (
        edge_term
        + jnp.dot(receiver, proc_w[1], preferred_element_type=jnp.float32)
        + jnp.dot(sender, proc_w[2], preferred_element_type=jnp.float32)
    )
    hidden = jax.nn.silu(pre).astype(jnp.bfloat16)
    edge_update = layer_norm(
        jnp.dot(hidden, proc_w[3], preferred_element_type=jnp.float32), gains[2]
    )
    edge_new = (edge_latent.astype(jnp.float32) + edge_update).astype(jnp.bfloat16)
    return (mesh_new, edge_new)


def solution(mesh):
    in_specs = (
        P(("band", "tile"), None),
        P(),
        P(),
        P(("band", "tile"), None),
        P(("band", "tile"), None),
        P(),
        P(),
        P(),
        P(),
        P(("band", "tile"), None, None),
        P(("band", "tile"), None, None),
        P(("band", "tile"), None),
        P(("band", "tile"), None, None),
        P(("band", "tile")),
        P(("band", "tile")),
    )
    out_specs = (P(("band", "tile"), None), P(("band", "tile"), None))
    return jax.shard_map(shards, mesh=mesh, in_specs=in_specs, out_specs=out_specs, check_vma=False)
```

profile of v0, /device:TPU:1, one launch (start us, length us, event | category | flops | bytes accessed | tf_op | source)
XLA Modules:
  0.0 243.4 jit_solution(1451078319391506276)
XLA Ops:
  0.6 0.0 copy-start
  0.6 1.5 copy-done
  2.2 7.8 %fusion.51 = (f32[4096]{0:T(1024)S(1)}, f32[4096,512]{0,1:T(8,128)}) fusion(bf16[512,512]{1,0:T(8,128)(2,1)} %param.17, bf16[4096,227]{0,1:T(8,128)(2,1)S(1)} %copy-done, bf16[227,512]{1,0:T(8,128)(2,1)} %param.16), kind=kOutput, calls=%fused_computation.74 | convolution fusion | flops 3112169472 | bytes 11021312 | tf_op jit(solution)/shard_map/dot_general | solution.py:42
  10.0 4.5 %multiply_reduce_fusion.1 = f32[4096]{0:T(1024)S(1)} fusion(f32[4096,512]{0,1:T(8,128)} %get-tuple-element.10, f32[4096]{0:T(1024)S(1)} %broadcast_multiply_fusion.1), kind=kLoop, calls=%fused_computation.10 | loop fusion | flops 6287360 | bytes 8421376 | tf_op jit(solution)/shard_map/reduce_sum | solution.py:10
  14.5 1.2 copy-done.5
  15.7 2.9 %multiply_convert_fusion.1 = bf16[4096,512]{0,1:T(8,128)(2,1)} fusion(f32[4096,512]{0,1:T(8,128)S(1)} %copy-done.5, f32[512]{0:T(512)S(1)} %bitcast.69, f32[4096]{0:T(1024)S(1)} %add_sqrt_fusion.1, f32[4096]{0:T(1024)S(1)} %broadcast_multiply_fusion.1), kind=kLoop, calls=%fused_computation.9 | loop fusion | flops 8388608 | bytes 12617728 | tf_op jit(solution)/shard_map/convert_element_type | solution.py:43
  18.6 6.5 %copy.29 = bf16[4096,512]{1,0:T(8,128)(2,1)} copy(bf16[4096,512]{0,1:T(8,128)(2,1)} %multiply_convert_fusion.1) | data formatting | bytes 8388608 | tf_op jit(solution)/shard_map/convert_element_type | solution.py:43
  25.1 0.1 copy.28
  25.2 0.1 reshape_squeeze.10
  25.3 12.0 %gather_fusion = bf16[2048,512]{1,0:T(8,128)(2,1)} fusion(bf16[4096,512]{1,0:T(8,128)(2,1)} %copy.29, s32[2048]{0:T(1024)S(1)} %broadcast_clamp_fusion.2), kind=kCustom, calls=%fused_computation | custom fusion | bytes 4202496 | tf_op jit(solution)/shard_map/gather | solution.py:44
  37.3 12.0 %all-to-all-start = ((bf16[128,16,512]{2,1,0:T(8,128)(2,1)}), bf16[128,16,512]{2,1,0:T(8,128)(2,1)}, u32[]{:S(2)}, u32[]{:S(2)}) async-start(bf16[128,16,512]{2,1,0:T(8,128)(2,1)} %bitcast.61), calls=%async_computation | async-start | bytes 4194304 | tf_op jit(solution)/shard_map/all_to_all | solution.py:45
  49.3 0.1 copy.27
  49.4 0.1 reshape_squeeze.9
  49.5 0.1 iota_compare_fusion
  49.6 0.1 lt.64
  49.7 2.8 %copy.26 = bf16[2560,512]{0,1:T(8,128)(2,1)} copy(bf16[2560,512]{1,0:T(8,128)(2,1)S(1)} %copy-done.3) | data formatting | bytes 5242880 | tf_op args[3]
  52.5 0.1 copy.32
  52.6 0.1 reshape_squeeze.11
  52.7 4.9 %fusion.25 = f32[2560,512]{1,0:T(8,128)} fusion(bf16[2560,512]{1,0:T(8,128)(2,1)S(1)} %copy-done.3, bf16[3,512,512]{2,1,0:T(8,128)(2,1)} %param.20), kind=kOutput, calls=%fused_computation.37 | convolution fusion | flops 1342177280 | bytes 8388608 | tf_op jit(solution)/shard_map/dot_general | solution.py:47
  57.6 12.0 %gather_fusion.1 = f32[2048,512]{1,0:T(8,128)} fusion(f32[2560,512]{1,0:T(8,128)} %fusion.25, s32[2048]{0:T(1024)S(1)} %broadcast_clamp_fusion.1), kind=kCustom, calls=%fused_computation.1 | custom fusion | bytes 8396800 | tf_op jit(solution)/shard_map/gather | solution.py:52
  69.6 4.9 %fusion.29 = f32[2560,512]{1,0:T(8,128)} fusion(bf16[2560,512]{1,0:T(8,128)(2,1)S(1)} %copy-done.3, bf16[3,512,512]{2,1,0:T(8,128)(2,1)} %param.21), kind=kOutput, calls=%fused_computation.40 | convolution fusion | flops 1342177280 | bytes 8388608 | tf_op jit(solution)/shard_map/dot_general | solution.py:48
  74.4 4.1 %all-to-all-done = bf16[128,16,512]{2,1,0:T(8,128)(2,1)} async-done(((bf16[128,16,512]{2,1,0:T(8,128)(2,1)}), bf16[128,16,512]{2,1,0:T(8,128)(2,1)}, u32[]{:S(2)}, u32[]{:S(2)}) %all-to-all-start) | async-done | bytes 2097184 | tf_op jit(solution)/shard_map/all_to_all | solution.py:45
  78.6 7.9 %fusion.13 = f32[2048,512]{1,0:T(8,128)} fusion(f32[2048,512]{1,0:T(8,128)} %gather_fusion.1, bf16[2048,512]{1,0:T(8,128)(2,1)} %bitcast.6, bf16[3,512,512]{2,1,0:T(8,128)(2,1)} %param.20), kind=kOutput, calls=%fused_computation.27 | convolution fusion | flops 2153775104 | bytes 11534336 | tf_op jit(solution)/shard_map/dot_general | solution.py:54
  86.5 17.1 %scatter_custom_fusion = f32[2560,512]{1,0:T(8,128)} fusion(s32[2048]{0:T(1024)S(1)} %bitcast.64, f32[2048,512]{1,0:T(8,128)} %fusion.13, f32[]{:T(128)} %constant.10.clone.1, pred[2048]{0:T(1024)(128)(4,1)S(1)} %lt.64), kind=kCustom, calls=%fused_computation.16 | custom fusion | flops 2097152 | bytes 9440256 | tf_op jit(solution)/shard_map/scatter-add | solution.py:58
  103.6 10.2 %fusion.52 = (f32[2560]{0:T(1024)S(1)}, f32[2560,512]{0,1:T(8,128)}) fusion(bf16[3,512,512]{2,1,0:T(8,128)(2,1)} %param.21, f32[2560,512]{1,0:T(8,128)} %fusion.29, f32[2560,512]{1,0:T(8,128)} %scatter_custom_fusion), kind=kOutput, calls=%fused_computation.75 | convolution fusion | flops 2694837760 | bytes 16787456 | tf_op jit(solution)/shard_map/dot_general | solution.py:64
  113.7 3.2 %multiply_reduce_fusion.2 = f32[2560]{0:T(1024)S(1)} fusion(f32[2560,512]{0,1:T(8,128)} %get-tuple-element.12, f32[2560]{0:T(1024)S(1)} %broadcast_multiply_fusion.2), kind=kLoop, calls=%fused_computation.13 | loop fusion | flops 3929600 | bytes 5263360 | tf_op jit(solution)/shard_map/reduce_sum | solution.py:10
  117.0 0.8 copy-done.7
  117.8 2.8 %add_convert_fusion.1 = bf16[2560,512]{0,1:T(8,128)(2,1)} fusion(bf16[2560,512]{0,1:T(8,128)(2,1)S(1)} %copy-done.8, f32[2560,512]{0,1:T(8,128)S(1)} %copy-done.7, f32[512]{0:T(512)S(1)} %bitcast.68, f32[2560]{0:T(1024)S(1)} %add_sqrt_fusion.2, f32[2560]{0:T(1024)S(1)} %broadcast_multiply_fusion.2), kind=kLoop, calls=%fused_computation.12 | loop fusion | flops 7864320 | bytes 10508288 | tf_op jit(solution)/shard_map/convert_element_type | solution.py:66
  120.6 3.0 %copy.36 = bf16[2560,512]{1,0:T(8,128)(2,1)S(1)} copy(bf16[2560,512]{0,1:T(8,128)(2,1)} %add_convert_fusion.1) | data formatting | bytes 5242880
  123.6 0.0 copy-start.2
  123.6 9.2 %gather_fusion.3 = bf16[2048,512]{1,0:T(8,128)(2,1)} fusion(bf16[2560,512]{1,0:T(8,128)(2,1)S(1)} %copy.36, s32[2048]{0:T(1024)S(1)} %broadcast_clamp_fusion), kind=kCustom, calls=%fused_computation.3 | custom fusion | bytes 4202496 | tf_op jit(solution)/shard_map/gather | solution.py:67
  132.8 6.1 %all-to-all-start.1 = ((bf16[128,16,512]{2,1,0:T(8,128)(2,1)}), bf16[128,16,512]{2,1,0:T(8,128)(2,1)}, u32[]{:S(2)}, u32[]{:S(2)}) async-start(bf16[128,16,512]{2,1,0:T(8,128)(2,1)} %bitcast.62), calls=%async_computation.1 | async-start | bytes 4194304 | tf_op jit(solution)/shard_map/all_to_all | solution.py:68
  138.9 0.0 copy-start.10
  138.9 0.0 copy-start.11
  138.9 6.3 %copy.30 = bf16[4096,512]{0,1:T(8,128)(2,1)} copy(bf16[4096,512]{1,0:T(8,128)(2,1)} %param.19) | data formatting | bytes 8388608 | tf_op args[4]
  145.3 7.9 %fusion.19 = f32[4096,512]{1,0:T(8,128)} fusion(bf16[4096,512]{1,0:T(8,128)(2,1)} %param.19, bf16[4,512,512]{2,1,0:T(8,128)(2,1)} %param.22), kind=kOutput, calls=%fused_computation.32 | convolution fusion | flops 2147483648 | bytes 13107200 | tf_op jit(solution)/shard_map/dot_general | solution.py:49
  153.2 17.3 %gather_fusion.2 = bf16[4096,512]{1,0:T(8,128)(2,1)} fusion(bf16[2560,512]{1,0:T(8,128)(2,1)S(1)} %copy.36, s32[4096]{0:T(1024)S(1)} %fusion.44), kind=kCustom, calls=%fused_computation.2 | custom fusion | bytes 8404992 | tf_op jit(solution)/shard_map/gather | solution.py:70
  170.5 7.9 %fusion.17 = f32[4096,512]{1,0:T(8,128)} fusion(bf16[4096,512]{1,0:T(8,128)(2,1)} %gather_fusion.2, bf16[4,512,512]{2,1,0:T(8,128)(2,1)} %param.22), kind=kOutput, calls=%fused_computation.30 | convolution fusion | flops 2147483648 | bytes 13107200 | tf_op jit(solution)/shard_map/dot_general | solution.py:74
  178.4 0.0 all-to-all-done.1
  178.4 4.1 %copy.34 = bf16[2048,512]{0,1:T(8,128)(2,1)} copy(bf16[2048,512]{1,0:T(8,128)(2,1)} %bitcast.17) | data formatting | bytes 4194304 | tf_op jit(solution)/shard_map/reshape | solution.py:69
  182.5 4.0 %pad_maximum_fusion = bf16[4608,512]{0,1:T(8,128)(2,1)} fusion(bf16[2048,512]{0,1:T(8,128)(2,1)} %copy.34, bf16[2560,512]{0,1:T(8,128)(2,1)S(1)} %copy-done.6), kind=kLoop, calls=%fused_computation.15 | loop fusion | flops 9437184 | bytes 9437184 | tf_op jit(solution)/shard_map/concatenate | solution.py:69
  186.5 6.7 %copy.35 = bf16[4608,512]{1,0:T(8,128)(2,1)} copy(bf16[4608,512]{0,1:T(8,128)(2,1)} %pad_maximum_fusion) | data formatting | bytes 9437184 | tf_op jit(solution)/shard_map/concatenate | solution.py:69
  193.2 20.5 %gather_fusion.4 = bf16[4096,512]{1,0:T(8,128)(2,1)} fusion(bf16[4608,512]{1,0:T(8,128)(2,1)} %copy.35, s32[4096]{0:T(1024)S(1)} %fusion.45), kind=kCustom, calls=%fused_computation.4 | custom fusion | bytes 8404992 | tf_op jit(solution)/shard_map/gather | solution.py:71
  213.7 12.0 %fusion.57 = (f32[4096]{0:T(1024)S(1)}, f32[4096,512]{0,1:T(8,128)}) fusion(bf16[4,512,512]{2,1,0:T(8,128)(2,1)S(1)} %copy-done.9, f32[4096,512]{1,0:T(8,128)} %fusion.19, f32[4096,512]{1,0:T(8,128)} %fusion.17, bf16[4096,512]{1,0:T(8,128)(2,1)} %gather_fusion.4), kind=kOutput, calls=%fused_computation.76 | convolution fusion | flops 4311740416 | bytes 30425088 | tf_op jit(solution)/shard_map/dot_general | solution.py:79
  225.7 4.5 %multiply_reduce_fusion = f32[4096]{0:T(1024)S(1)} fusion(f32[4096,512]{0,1:T(8,128)} %get-tuple-element.14, f32[4096]{0:T(1024)S(1)} %broadcast_multiply_fusion), kind=kLoop, calls=%fused_computation.7 | loop fusion | flops 6287360 | bytes 8421376 | tf_op jit(solution)/shard_map/reduce_sum | solution.py:10
  230.3 1.2 copy-done.4
  231.5 5.5 %add_convert_fusion = bf16[4096,512]{0,1:T(8,128)(2,1)} fusion(bf16[4096,512]{0,1:T(8,128)(2,1)} %copy.30, f32[4096,512]{0,1:T(8,128)S(1)} %copy-done.4, f32[512]{0:T(512)S(1)} %bitcast.67, f32[4096]{0:T(1024)S(1)} %add_sqrt_fusion, f32[4096]{0:T(1024)S(1)} %broadcast_multiply_fusion), kind=kLoop, calls=%fused_computation.6 | loop fusion | flops 12582912 | bytes 16812032 | tf_op jit(solution)/shard_map/convert_element_type | solution.py:81
  237.0 6.4 %copy.37 = bf16[4096,512]{1,0:T(8,128)(2,1)} copy(bf16[4096,512]{0,1:T(8,128)(2,1)} %add_convert_fusion) | data formatting | bytes 8388608
  (41 shorter events, 0.2 us)
Async XLA Ops:
  0.6 1.5 copy-start
  9.9 4.5 %copy-start.15 = (f32[3,512]{1,0:T(4,128)S(1)}, f32[3,512]{1,0:T(4,128)}, u32[]{:S(2)}) copy-start(f32[3,512]{1,0:T(4,128)} %param.23) | copy-start | bytes 18436
  9.9 5.8 %copy-start.5 = (f32[4096,512]{0,1:T(8,128)S(1)}, f32[4096,512]{0,1:T(8,128)}, u32[]{:S(2)}) copy-start(f32[4096,512]{0,1:T(8,128)} %get-tuple-element.10) | copy-start | bytes 25165828
  18.6 6.5 %copy-start.12 = (s32[1,128,16]{1,2,0:T(8,128)S(1)}, s32[1,128,16]{1,2,0:T(8,128)}, u32[]{:S(2)}) copy-start(s32[1,128,16]{1,2,0:T(8,128)} %param.24) | copy-start | bytes 24580
  37.3 12.0 %copy-start.13 = (s32[1,128,16]{1,2,0:T(8,128)S(1)}, s32[1,128,16]{1,2,0:T(8,128)}, u32[]{:S(2)}) copy-start(s32[1,128,16]{1,2,0:T(8,128)} %param.25) | copy-start | bytes 24580
  37.3 12.2 %copy-start.16 = (s32[1,128]{1,0:T(1,128)S(1)}, s32[1,128]{1,0:T(1,128)}, u32[]{:S(2)}) copy-start(s32[1,128]{1,0:T(1,128)} %param.26) | copy-start | bytes 1540
  37.3 12.4 %copy-start.3 = (bf16[2560,512]{1,0:T(8,128)(2,1)S(1)}, bf16[2560,512]{1,0:T(8,128)(2,1)}, u32[]{:S(2)}) copy-start(bf16[2560,512]{1,0:T(8,128)(2,1)} %param.18) | copy-start | bytes 7864324
  37.3 15.2 %copy-start.14 = (s32[1,128,16]{1,2,0:T(8,128)S(1)}, s32[1,128,16]{1,2,0:T(8,128)}, u32[]{:S(2)}) copy-start(s32[1,128,16]{1,2,0:T(8,128)} %param.27) | copy-start | bytes 24580
  37.3 41.3 %all-to-all-start = ((bf16[128,16,512]{2,1,0:T(8,128)(2,1)}), bf16[128,16,512]{2,1,0:T(8,128)(2,1)}, u32[]{:S(2)}, u32[]{:S(2)}) async-start(bf16[128,16,512]{2,1,0:T(8,128)(2,1)} %bitcast.61), calls=%async_computation | async-start | bytes 4194304 | tf_op jit(solution)/shard_map/all_to_all | solution.py:45
  103.6 13.4 %copy-start.8 = (bf16[2560,512]{0,1:T(8,128)(2,1)S(1)}, bf16[2560,512]{0,1:T(8,128)(2,1)}, u32[]{:S(2)}) copy-start(bf16[2560,512]{0,1:T(8,128)(2,1)} %copy.26) | copy-start | bytes 7864324
  113.7 4.0 %copy-start.7 = (f32[2560,512]{0,1:T(8,128)S(1)}, f32[2560,512]{0,1:T(8,128)}, u32[]{:S(2)}) copy-start(f32[2560,512]{0,1:T(8,128)} %get-tuple-element.12) | copy-start | bytes 15728644
  123.6 29.6 %copy-start.2 = (bf16[2560,512]{1,0:T(8,128)(2,1)}, bf16[2560,512]{1,0:T(8,128)(2,1)S(1)}, u32[]{:S(2)}) copy-start(bf16[2560,512]{1,0:T(8,128)(2,1)S(1)} %copy.36) | copy-start | bytes 7864324
  132.8 45.6 %all-to-all-start.1 = ((bf16[128,16,512]{2,1,0:T(8,128)(2,1)}), bf16[128,16,512]{2,1,0:T(8,128)(2,1)}, u32[]{:S(2)}, u32[]{:S(2)}) async-start(bf16[128,16,512]{2,1,0:T(8,128)(2,1)} %bitcast.62), calls=%async_computation.1 | async-start | bytes 4194304 | tf_op jit(solution)/shard_map/all_to_all | solution.py:68
  138.9 6.4 %copy-start.10 = (s32[4096]{0:T(1024)S(1)}, s32[4096]{0:T(1024)}, u32[]{:S(2)}) copy-start(s32[4096]{0:T(1024)} %param.29) | copy-start | bytes 49156
  138.9 6.4 %copy-start.11 = (s32[4096]{0:T(1024)S(1)}, s32[4096]{0:T(1024)}, u32[]{:S(2)}) copy-start(s32[4096]{0:T(1024)} %param.28) | copy-start | bytes 49156
  178.4 4.1 %copy-start.6 = (bf16[2560,512]{0,1:T(8,128)(2,1)S(1)}, bf16[2560,512]{0,1:T(8,128)(2,1)}, u32[]{:S(2)}) copy-start(bf16[2560,512]{0,1:T(8,128)(2,1)} %add_convert_fusion.1) | copy-start | bytes 7864324
  193.2 20.5 %copy-start.9 = (bf16[4,512,512]{2,1,0:T(8,128)(2,1)S(1)}, bf16[4,512,512]{2,1,0:T(8,128)(2,1)}, u32[]{:S(2)}) copy-start(bf16[4,512,512]{2,1,0:T(8,128)(2,1)} %param.22) | copy-start | bytes 6291460
  225.7 5.8 %copy-start.4 = (f32[4096,512]{0,1:T(8,128)S(1)}, f32[4096,512]{0,1:T(8,128)}, u32[]{:S(2)}) copy-start(f32[4096,512]{0,1:T(8,128)} %get-tuple-element.14) | copy-start | bytes 25165828
  231.5 11.9 %copy-start.1 = (bf16[4096,227]{0,1:T(8,128)(2,1)S(1)}, bf16[4096,227]{0,1:T(8,128)(2,1)}, u32[]{:S(2)}) copy-start(bf16[4096,227]{0,1:T(8,128)(2,1)} %param.15) | copy-start | bytes 5578756
where the time goes:
time: 244 us; the launch traced here: 243 us
  local copies, waits for them, and re-layouts  112 us (46%)
  matrix products  63.3 us (26%)
  other arithmetic  44.7 us (18%)
  starting transfers between devices  18.1 us (7%)
  waiting for transfers between devices  4.14 us (2%)
    unnamed x41, local copies, waits for them, and re-layouts  23.6 us
    gather x1, local copies, waits for them, and re-layouts, shards(): sender = table[proc_src]  20.5 us
    gather x1, local copies, waits for them, and re-layouts, shards(): receiver = mesh_new[proc_dst]  17.3 us
    scatter-add x1, other arithmetic, shards(): jnp.zeros((mesh_rows, width), jnp.float32).at[dst_flat].add(message)  17.1 us
    reduce_sum x3, other arithmetic, layer_norm(): variance = jnp.mean(centred * centred, axis=-1, keepdims=True)  12.2 us
    dot_general x1, matrix products, shards(): jnp.dot(hidden, proc_w[3], preferred_element_type=jnp.float32)  12 us
    gather x1, local copies, waits for them, and re-layouts, shards(): outgoing = grid_latent[g2m_src[0].reshape(-1)].reshape(peers, slots, width)  12 us
    all_to_all x1, starting transfers between devices, shards(): lax.all_to_all(outgoing, ('band', 'tile'), split_axis=0, concat_axis=0, t...  12 us
  transfers between devices with their start and end apart: 2, of which 1 were waited for; matrix products, arithmetic and copies ran while one was open for 26% of the time, Pallas kernels for 0%

commit v1 on v0

v1 whole, which is shorter than its diff:
```python
import functools

import jax
import jax.numpy as jnp
from jax import lax
from jax.experimental import pallas as pl
from jax.experimental.pallas import tpu as pltpu
from jax.sharding import PartitionSpec as P

F32 = jnp.float32
BF16 = jnp.bfloat16
VMEM = pl.BlockSpec(memory_space=pltpu.VMEM)
SMEM = pl.BlockSpec(memory_space=pltpu.SMEM)
PARAMS = pltpu.CompilerParams(vmem_limit_bytes=52 * 2**20)
UNROLL = 32


def dot(a, b):
    return jnp.dot(a, b, preferred_element_type=F32)


def silu(v):
    half = 0.5 * v
    return half + half * jnp.tanh(half)


def norm(value, gain):
    mean = jnp.mean(value, axis=-1, keepdims=True)
    centred = value - mean
    variance = jnp.mean(centred * centred, axis=-1, keepdims=True)
    return centred * lax.rsqrt(variance + 1e-05) * gain


def put_rows(table, start, value):
    rows, width = value.shape
    parts = -(-width // 128)
    for part in range(parts):
        top = min(width, part * 128 + 128)
        table[pl.ds(start * parts + part, rows, stride=parts), : top - part * 128] = value[
            :, part * 128 : top
        ]


def get_part(table, start, rows, part, parts):
    return table[pl.ds(start * parts + part, rows, stride=parts), :]


def get_rows(table, start, rows, parts):
    return jnp.concatenate(
        [get_part(table, start, rows, part, parts) for part in range(parts)], axis=1
    )


def copy_rows(index, table, target, start, base, rows, parts):
    @pl.loop(0, rows // UNROLL)
    def _(block):
        for inner in range(UNROLL):
            row = block * UNROLL + inner
            source = pl.multiple_of(index[start + row], parts)
            target[pl.ds(pl.multiple_of((base + row) * parts, parts), parts), :] = table[
                pl.ds(source, parts), :
            ]


def pick_grid(index, grid, out, table, picked):
    rows, width = grid.shape
    slots = out.shape[0]
    step = 128

    @pl.loop(0, rows // step)
    def _(block):
        at = pl.multiple_of(block * step, step)
        put_rows(table, at, grid[pl.ds(at, step), :].astype(F32))

    @pl.loop(0, slots // step)
    def _(block):
        at = pl.multiple_of(block * step, step)
        copy_rows(index, table, picked, at, at, step, 2)
        value = get_rows(picked, at, step, 2)
        out[pl.ds(at, step), :] = value[:, :width].astype(BF16)


def mesh_side(index, mesh, w_mesh, w_own, out, own, table):
    rows = mesh.shape[0]
    slots = out.shape[0] // 4
    step = 256

    @pl.loop(0, rows // step)
    def _(block):
        at = pl.multiple_of(block * step, step)
        value = mesh[pl.ds(at, step), :]
        put_rows(table, at, dot(value, w_mesh[...]))
        own[pl.ds(at, step), :] = dot(value, w_own[...])

    copy_rows(index, table, out, 0, 0, slots, 4)


def encode(
    halo_index, rows_in, target, mesh_term, own, mesh, embed_in, embed_out, enc_w, node_w, gains,
    mesh_out, halo_out, hidden, table, picked,
):
    slots, width = rows_in.shape
    mesh_rows = mesh.shape[0]
    step = 256

    @pl.loop(0, slots // step)
    def _(block):
        at = pl.multiple_of(block * step, step)
        first = silu(dot(rows_in[pl.ds(at, step), :], embed_in[...])).astype(BF16)
        latent = norm(dot(first, embed_out[...]), gains[0:1, :]).astype(BF16)
        pre = dot(latent, enc_w[0]) + get_rows(mesh_term, at, step, 4)
        hidden[pl.ds(at, step), :] = silu(pre).astype(BF16)

    block_rows = 640

    @pl.loop(0, mesh_rows // block_rows)
    def _(block):
        at = pl.multiple_of(block * block_rows, block_rows)
        row = lax.broadcasted_iota(jnp.int32, (block_rows, slots), 0) + at
        mask = jnp.where(row == target[...], F32(1.0), F32(0.0)).astype(BF16)
        summed = dot(mask, hidden[...]).astype(BF16)
        aggregate = dot(summed, enc_w[2]).astype(BF16)
        node = silu(own[pl.ds(at, block_rows), :] + dot(aggregate, node_w[1])).astype(BF16)
        update = norm(dot(node, node_w[2]), gains[1:2, :])
        new = (mesh[pl.ds(at, block_rows), :].astype(F32) + update).astype(BF16)
        mesh_out[pl.ds(at, block_rows), :] = new
        put_rows(table, at, new.astype(F32))

    halo_slots = halo_out.shape[0]
    step = 128

    @pl.loop(0, halo_slots // step)
    def _(block):
        at = pl.multiple_of(block * step, step)
        copy_rows(halo_index, table, picked, at, at, step, 4)
        halo_out[pl.ds(at, step), :] = get_rows(picked, at, step, 4).astype(BF16)


def local_terms(dst, src, mesh, proc_w, edges, out, receivers, senders, picked):
    rows = mesh.shape[0]
    block_rows = edges.shape[0]
    step = 256
    grid_step = pl.program_id(0)

    @pl.when(grid_step == 0)
    def _():
        @pl.loop(0, rows // step)
        def _(block):
            at = pl.multiple_of(block * step, step)
            value = mesh[pl.ds(at, step), :]
            put_rows(receivers, at, dot(value, proc_w[1]))
            put_rows(senders, at, dot(value, proc_w[2]))

        senders[pl.ds(rows * 4, 8), :] = jnp.zeros((8, 128), F32)

    start = grid_step * block_rows

    @pl.loop(0, block_rows // UNROLL)
    def _(block):
        for inner in range(UNROLL):
            row = block * UNROLL + inner
            one = pl.multiple_of(dst[start + row], 4)
            two = pl.multiple_of(src[start + row], 4)
            picked[pl.ds(pl.multiple_of(row * 4, 4), 4), :] = (
                receivers[pl.ds(one, 4), :] + senders[pl.ds(two, 4), :]
            )

    out[...] = dot(edges[...], proc_w[0]) + get_rows(picked, 0, block_rows, 4)


def edge_update(src, halo, proc_w, edges, local, gains, out, senders, picked):
    rows = halo.shape[0]
    block_rows = edges.shape[0]
    step = 256
    grid_step = pl.program_id(0)

    @pl.when(grid_step == 0)
    def _():
        @pl.loop(0, rows // step)
        def _(block):
            at = pl.multiple_of(block * step, step)
            put_rows(senders, at, dot(halo[pl.ds(at, step), :], proc_w[2]))

        senders[pl.ds(rows * 4, 8), :] = jnp.zeros((8, 128), F32)

    copy_rows(src, senders, picked, grid_step * block_rows, 0, block_rows, 4)
    pre = local[...] + get_rows(picked, 0, block_rows, 4)
    hidden = silu(pre).astype(BF16)
    update = norm(dot(hidden, proc_w[3]), gains[2:3, :])
    out[...] = (edges[...].astype(F32) + update).astype(BF16)


def shards(
    grid_in,
    embed_in,
    embed_out,
    mesh_latent,
    edge_latent,
    enc_w,
    node_w,
    proc_w,
    gains,
    g2m_src,
    g2m_dst,
    g2m_count,
    halo_rows,
    proc_dst,
    proc_src,
):
    axes = ("band", "tile")
    peers = lax.axis_size("band") * lax.axis_size("tile")
    grid_rows, features = grid_in.shape
    mesh_rows, width = mesh_latent.shape
    edges = edge_latent.shape[0]
    cap = g2m_src.shape[2]
    halo_cap = halo_rows.shape[2]
    slots = peers * cap
    halo_slots = peers * halo_cap
    parts = width // 128

    def full(rows, columns, dtype):
        return jax.ShapeDtypeStruct((rows, columns), dtype)

    def cost(flops, moved):
        return pl.CostEstimate(flops=flops, bytes_accessed=moved, transcendentals=0)

    outgoing = pl.pallas_call(
        pick_grid,
        out_shape=full(slots, features, BF16),
        in_specs=[SMEM, VMEM],
        out_specs=VMEM,
        scratch_shapes=[pltpu.VMEM((grid_rows * 2, 128), F32), pltpu.VMEM((slots * 2, 128), F32)],
        compiler_params=PARAMS,
        name="pick_grid",
    )(g2m_src[0].reshape(-1) * 2, grid_in)
    arrived = lax.all_to_all(
        outgoing.reshape(peers, cap, features), axes, split_axis=0, concat_axis=0, tiled=True
    ).reshape(slots, features)

    dst_flat = g2m_dst[0].reshape(-1)
    mesh_term, own = pl.pallas_call(
        mesh_side,
        out_shape=(full(slots * parts, 128, F32), full(mesh_rows, width, F32)),
        in_specs=[SMEM, VMEM, VMEM, VMEM],
        out_specs=(VMEM, VMEM),
        scratch_shapes=[pltpu.VMEM((mesh_rows * parts, 128), F32)],
        compiler_params=PARAMS,
        cost_estimate=cost(10**10, 2 * 10**7),
        name="mesh_side",
    )(dst_flat * parts, mesh_latent, enc_w[1], node_w[0])

    live = (jnp.arange(cap, dtype=jnp.int32)[None, :] < g2m_count[0][:, None]).reshape(-1)
    target = jnp.where(live, dst_flat, -1).reshape(1, slots)
    mesh_new, halo_out = pl.pallas_call(
        encode,
        out_shape=(full(mesh_rows, width, BF16), full(halo_slots, width, BF16)),
        in_specs=[SMEM] + [VMEM] * 10,
        out_specs=(VMEM, VMEM),
        scratch_shapes=[
            pltpu.VMEM((slots, width), BF16),
            pltpu.VMEM((mesh_rows * parts, 128), F32),
            pltpu.VMEM((halo_slots * parts, 128), F32),
        ],
        compiler_params=PARAMS,
        name="encode",
    )(
        halo_rows[0].reshape(-1) * parts, arrived, target, mesh_term, own, mesh_latent,
        embed_in, embed_out, enc_w, node_w, gains,
    )
    halo_in = lax.all_to_all(
        halo_out.reshape(peers, halo_cap, width), axes, split_axis=0, concat_axis=0, tiled=True
    ).reshape(halo_slots, width)

    block_rows = 512
    block = pl.BlockSpec((block_rows, width), lambda i, *_: (i, 0))
    picked = pltpu.VMEM((block_rows * parts, 128), F32)
    remote = proc_src >= mesh_rows
    local = pl.pallas_call(
        local_terms,
        out_shape=full(edges, width, F32),
        grid=(edges // block_rows,),
        in_specs=[SMEM, SMEM, VMEM, VMEM, block],
        out_specs=block,
        scratch_shapes=[
            pltpu.VMEM((mesh_rows * parts, 128), F32),
            pltpu.VMEM((mesh_rows * parts + 8, 128), F32),
            picked,
        ],
        compiler_params=PARAMS,
        cost_estimate=cost(2 * 10**10, 4 * 10**7),
        name="local_terms",
    )(
        proc_dst * parts,
        jnp.where(remote, mesh_rows, proc_src) * parts,
        mesh_new,
        proc_w,
        edge_latent,
    )
    edge_new = pl.pallas_call(
        edge_update,
        out_shape=full(edges, width, BF16),
        grid=(edges // block_rows,),
        in_specs=[SMEM, VMEM, VMEM, block, block, VMEM],
        out_specs=block,
        scratch_shapes=[pltpu.VMEM((halo_slots * parts + 8, 128), F32), picked],
        compiler_params=PARAMS,
        name="edge_update",
    )(
        jnp.where(remote, proc_src - mesh_rows, halo_slots) * parts,
        halo_in,
        proc_w,
        edge_latent,
        local,
        gains,
    )
    return (mesh_new, edge_new)


def solution(mesh):
    rows = P(("band", "tile"), None)
    slots = P(("band", "tile"), None, None)
    flat = P(("band", "tile"))
    in_specs = (
        rows, P(), P(), rows, rows, P(), P(), P(), P(), slots, slots, rows, slots, flat, flat,
    )
    return jax.shard_map(
        shards, mesh=mesh, in_specs=in_specs, out_specs=(rows, rows), check_vma=False
    )
```

time: 244 us -> 125 us (0.51)
  local copies, waits for them, and re-layouts: 112 us -> 6.13 us
  Pallas kernels: 0 us -> 84 us
  matrix products: 63.3 us -> 0 us
  other arithmetic: 44.7 us -> 0.82 us
  waiting for transfers between devices: 4.14 us -> 15 us
    pallas_call x0 -> x5, Pallas kernels: none -> 84 us  [the longest x1 29.8 us: shards(): pl.pallas_call(encode, out_shape=(full(mesh_rows, width, BF16), full(halo...]
    gather x5 -> x0, local copies, waits for them, and re-layouts: 71 us -> none  [the longest x1 20.5 us: shards(): sender = table[proc_src]]
    dot_general x8 -> x0, matrix products: 63.3 us -> none  [the longest x1 12 us: shards(): jnp.dot(hidden, proc_w[3], preferred_element_type=jnp.float32)]
    unnamed x41 -> x18, local copies, waits for them, and re-layouts: 23.6 us -> 4.12 us
    scatter-add x1 -> x0, other arithmetic: 17.1 us -> none  [shards(): jnp.zeros((mesh_rows, width), jnp.float32).at[dst_flat].add(message)]
    reduce_sum x3 -> x0, other arithmetic: 12.2 us -> none  [layer_norm(): variance = jnp.mean(centred * centred, axis=-1, keepdims=True)]
    convert_element_type x3 -> x0, other arithmetic: 11.2 us -> none  [the longest x1 5.5 us: shards(): (edge_latent.astype(jnp.float32) + edge_update).astype(jnp.bfloat16)]
    all_to_all x2, waiting for transfers between devices: 4.14 us -> 15 us  [the longest x1 10.3 us: shards(): lax.all_to_all(halo_out.reshape(peers, halo_cap, width), axes, split_axis...]
  transfers between devices with their start and end apart: 2 -> 2, of which waited for: 1 -> 2; matrix products, arithmetic and copies ran while one was open for 26% -> 2% of each run, Pallas kernels for 0% -> 25%
where the time goes in v1:
time: 125 us; the launch traced here: 124 us
  Pallas kernels  84 us (67%)
  starting transfers between devices  17.6 us (14%)
  waiting for transfers between devices  15 us (12%)
  local copies, waits for them, and re-layouts  6.13 us (5%)
    pallas_call x1, Pallas kernels, shards(): pl.pallas_call(encode, out_shape=(full(mesh_rows, width, BF16), full(halo...  29.8 us
    pallas_call x1, Pallas kernels, shards(): pl.pallas_call(local_terms, out_shape=full(edges, width, F32), grid=(edge...  19.1 us
    pallas_call x1, Pallas kernels, shards(): pl.pallas_call(edge_update, out_shape=full(edges, width, BF16), grid=(edg...  17.5 us
    pallas_call x1, Pallas kernels, shards(): pl.pallas_call(mesh_side, out_shape=(full(slots * parts, 128, F32), full(...  11.8 us
    all_to_all x1, starting transfers between devices, shards(): lax.all_to_all(outgoing.reshape(peers, cap, features), axes, split_axis=0...  11.5 us
    all_to_all x1, waiting for transfers between devices, shards(): lax.all_to_all(halo_out.reshape(peers, halo_cap, width), axes, split_axis...  10.3 us
    all_to_all x1, starting transfers between devices, shards(): lax.all_to_all(halo_out.reshape(peers, halo_cap, width), axes, split_axis...  6.13 us
    pallas_call x1, Pallas kernels, shards(): pl.pallas_call(pick_grid, out_shape=full(slots, features, BF16), in_specs...  5.7 us
  transfers between devices with their start and end apart: 2, of which 2 were waited for; matrix products, arithmetic and copies ran while one was open for 2% of the time, Pallas kernels for 25%

profile of v1, /device:TPU:1, one launch (start us, length us, event | category | flops | bytes accessed | tf_op | source)
XLA Modules:
  0.0 124.3 jit_solution(17973605205412458903)
XLA Ops:
  0.6 0.7 broadcast_multiply_fusion.1
  1.3 0.1 copy.20
  1.4 0.1 mul.31.index
  1.5 4.0 %copy.21.grid = bf16[4096,227]{1,0:T(8,128)(2,1)} copy(bf16[4096,227]{0,1:T(8,128)(2,1)} %param.15) | data formatting | bytes 3719168 | tf_op args[0]
  5.5 0.0 copy-start.3
  5.5 0.0 copy-start.6
  5.5 0.0 copy-start.7
  5.5 0.0 copy-start.4
  5.5 5.7 %pick_grid.1 = bf16[2048,227]{1,0:T(8,128)(2,1)} custom-call(s32[2048]{0:T(1024)S(1)} %mul.31.index, bf16[4096,227]{1,0:T(8,128)(2,1)} %copy.21.grid), custom_call_target="tpu_custom_call" | custom-call | tf_op jit(solution)/shard_map/pick_grid/pallas_call | solution.py:227
  11.2 11.5 %all-to-all-start = ((bf16[128,16,227]{2,1,0:T(8,128)(2,1)}), bf16[128,16,227]{2,1,0:T(8,128)(2,1)S(1)}, u32[]{:S(2)}, u32[]{:S(2)}) async-start(bf16[128,16,227]{2,1,0:T(8,128)(2,1)} %bitcast), calls=%async_computation | async-start | bytes 2097152 | tf_op jit(solution)/shard_map/all_to_all | solution.py:236
  22.7 0.0 copy-done.3
  22.7 0.1 copy.22
  22.8 0.0 copy-done.6
  22.8 0.0 copy-done.7
  22.9 0.1 iota_compare_fusion
  22.9 0.1 lt.30
  23.0 0.0 copy-done.4
  23.1 0.1 copy.23
  23.2 0.1 mul.33.index
  23.3 0.1 copy.19
  23.4 0.1 mul.28.halo_index
  23.4 0.1 reshape_squeeze.2
  23.6 1.3 %slice_bitcast_fusion = (bf16[512,512]{1,0:T(8,128)(2,1)S(1)}, bf16[512,512]{1,0:T(8,128)(2,1)S(1)}) fusion(bf16[3,512,512]{2,1,0:T(8,128)(2,1)} %node_w.1, bf16[3,512,512]{2,1,0:T(8,128)(2,1)} %enc_w.1), kind=kLoop, calls=%fused_computation | loop fusion | bytes 2097152 | tf_op jit(solution)/shard_map/squeeze | solution.py:250
  24.8 0.0 copy-start
  24.8 0.0 copy-start.1
  24.9 0.0 copy-start.2
  24.9 11.8 %mesh_side.1 = (f32[8192,128]{1,0:T(8,128)}, f32[2560,512]{1,0:T(8,128)}) custom-call(s32[2048]{0:T(1024)S(1)} %mul.33.index, bf16[2560,512]{1,0:T(8,128)(2,1)} %mesh.3, bf16[512,512]{1,0:T(8,128)(2,1)S(1)} %get-tuple-element.13.w_mesh, bf16[512,512]{1,0:T(8,128)(2,1)S(1)} %get-tuple-element.12.w_own), custom_call_target="tpu_custom_call" | custom-call | flops 10000000000 | bytes 20000000 | tf_op jit(solution)/shard_map/mesh_side/pallas_call | solution.py:241
  36.7 4.6 %all-to-all-done = bf16[128,16,227]{2,1,0:T(8,128)(2,1)S(1)} async-done(((bf16[128,16,227]{2,1,0:T(8,128)(2,1)}), bf16[128,16,227]{2,1,0:T(8,128)(2,1)S(1)}, u32[]{:S(2)}, u32[]{:S(2)}) %all-to-all-start) | async-done | bytes 929824 | tf_op jit(solution)/shard_map/all_to_all | solution.py:236
  41.3 0.0 copy-done
  41.3 0.0 copy-done.1
  41.3 0.0 copy-done.2
  41.3 29.8 %encode.1 = (bf16[2560,512]{1,0:T(8,128)(2,1)}, bf16[2048,512]{1,0:T(8,128)(2,1)}) custom-call(s32[2048]{0:T(1024)S(1)} %mul.28.halo_index, bf16[2048,227]{1,0:T(8,128)(2,1)S(1)} %bitcast.9, s32[1,2048]{1,0:T(1,128)S(1)} %broadcast_select_fusion.target, f32[8192,128]{1,0:T(8,128)} %get-tuple-element.6.mesh_term, f32[2560,512]{1,0:T(8,128)} %get-tuple-element.7.own, ...), custom_call_target="tpu_custom_call" | custom-call | tf_op jit(solution)/shard_map/encode/pallas_call | solution.py:254
  71.2 0.0 copy-start.5
  71.2 6.1 %all-to-all-start.1 = ((bf16[128,16,512]{2,1,0:T(8,128)(2,1)}), bf16[128,16,512]{2,1,0:T(8,128)(2,1)}, u32[]{:S(2)}, u32[]{:S(2)}) async-start(bf16[128,16,512]{2,1,0:T(8,128)(2,1)} %bitcast.10), calls=%async_computation.1 | async-start | bytes 4194304 | tf_op jit(solution)/shard_map/all_to_all | solution.py:270
  77.3 0.0 copy-done.5
  77.3 19.1 %local_terms.1.local = f32[4096,512]{1,0:T(8,128)} custom-call(s32[4096]{0:T(1024)S(1)} %broadcast_multiply_fusion.dst, s32[4096]{0:T(1024)S(1)} %get-tuple-element.10.src, bf16[2560,512]{1,0:T(8,128)(2,1)} %get-tuple-element.4.mesh, bf16[4,512,512]{2,1,0:T(8,128)(2,1)} %proc_w.3, bf16[4096,512]{1,0:T(8,128)(2,1)} %edges.3), custom_call_target="tpu_custom_call" | custom-call | flops 20000000000 | bytes 40000000 | tf_op jit(solution)/shard_map/local_terms/pallas_call | solution.py:278
  96.4 10.3 %all-to-all-done.1 = bf16[128,16,512]{2,1,0:T(8,128)(2,1)} async-done(((bf16[128,16,512]{2,1,0:T(8,128)(2,1)}), bf16[128,16,512]{2,1,0:T(8,128)(2,1)}, u32[]{:S(2)}, u32[]{:S(2)}) %all-to-all-start.1) | async-done | bytes 2097184 | tf_op jit(solution)/shard_map/all_to_all | solution.py:270
  106.8 17.5 %edge_update.1 = bf16[4096,512]{1,0:T(8,128)(2,1)} custom-call(s32[4096]{0:T(1024)S(1)} %get-tuple-element.11.src, bf16[2048,512]{1,0:T(8,128)(2,1)} %bitcast.6.halo, bf16[4,512,512]{2,1,0:T(8,128)(2,1)} %proc_w.3, bf16[4096,512]{1,0:T(8,128)(2,1)} %edges.3, f32[4096,512]{1,0:T(8,128)} %local_terms.1.local, f32[3,512]{1,0:T(4,128)S(1)} %copy-done.2), custom_call_target="tpu_custom_call" | custom-call | tf_op jit(solution)/shard_map/edge_update/pallas_call | solution.py:299
  (5 shorter events, 0.0 us)
Async XLA Ops:
  5.5 17.2 %copy-start.3 = (s32[1,128,16]{1,2,0:T(8,128)S(1)}, s32[1,128,16]{1,2,0:T(8,128)}, u32[]{:S(2)}) copy-start(s32[1,128,16]{1,2,0:T(8,128)} %param.25) | copy-start | bytes 24580
  5.5 17.3 %copy-start.6 = (s32[1,128,16]{1,2,0:T(8,128)S(1)}, s32[1,128,16]{1,2,0:T(8,128)}, u32[]{:S(2)}) copy-start(s32[1,128,16]{1,2,0:T(8,128)} %param.27) | copy-start | bytes 24580
  5.5 17.4 %copy-start.7 = (s32[1,128]{1,0:T(1,128)S(1)}, s32[1,128]{1,0:T(1,128)}, u32[]{:S(2)}) copy-start(s32[1,128]{1,0:T(1,128)} %param.26) | copy-start | bytes 1540
  5.5 17.6 %copy-start.4 = (s32[4096]{0:T(1024)S(1)}, s32[4096]{0:T(1024)}, u32[]{:S(2)}) copy-start(s32[4096]{0:T(1024)} %param.29) | copy-start | bytes 49156
  11.2 30.1 %all-to-all-start = ((bf16[128,16,227]{2,1,0:T(8,128)(2,1)}), bf16[128,16,227]{2,1,0:T(8,128)(2,1)S(1)}, u32[]{:S(2)}, u32[]{:S(2)}) async-start(bf16[128,16,227]{2,1,0:T(8,128)(2,1)} %bitcast), calls=%async_computation | async-start | bytes 2097152 | tf_op jit(solution)/shard_map/all_to_all | solution.py:236
  24.8 16.5 %copy-start = (bf16[512,512]{1,0:T(8,128)(2,1)S(1)}, bf16[512,512]{1,0:T(8,128)(2,1)}, u32[]{:S(2)}) copy-start(bf16[512,512]{1,0:T(8,128)(2,1)} %embed_out.1) | copy-start | bytes 1572868
  24.8 16.5 %copy-start.1 = (bf16[227,512]{1,0:T(8,128)(2,1)S(1)}, bf16[227,512]{1,0:T(8,128)(2,1)}, u32[]{:S(2)}) copy-start(bf16[227,512]{1,0:T(8,128)(2,1)} %embed_in.1) | copy-start | bytes 697348
  24.9 16.5 %copy-start.2 = (f32[3,512]{1,0:T(4,128)S(1)}, f32[3,512]{1,0:T(4,128)}, u32[]{:S(2)}) copy-start(f32[3,512]{1,0:T(4,128)} %gains.3) | copy-start | bytes 18436
  71.2 6.1 %copy-start.5 = (s32[4096]{0:T(1024)S(1)}, s32[4096]{0:T(1024)}, u32[]{:S(2)}) copy-start(s32[4096]{0:T(1024)} %param.28) | copy-start | bytes 49156
  71.2 35.6 %all-to-all-start.1 = ((bf16[128,16,512]{2,1,0:T(8,128)(2,1)}), bf16[128,16,512]{2,1,0:T(8,128)(2,1)}, u32[]{:S(2)}, u32[]{:S(2)}) async-start(bf16[128,16,512]{2,1,0:T(8,128)(2,1)} %bitcast.10), calls=%async_computation.1 | async-start | bytes 4194304 | tf_op jit(solution)/shard_map/all_to_all | solution.py:270

commit v2 on v1

v2 whole, which is shorter than its diff:
```python
import jax
import jax.numpy as jnp
from jax import lax
from jax.experimental import pallas as pl
from jax.experimental.pallas import tpu as pltpu
from jax.sharding import PartitionSpec as P

F32 = jnp.float32
BF16 = jnp.bfloat16
VMEM = pl.BlockSpec(memory_space=pltpu.VMEM)
SMEM = pl.BlockSpec(memory_space=pltpu.SMEM)
ANY = pl.BlockSpec(memory_space=pl.ANY)
STEP = 256


def params(mebibytes):
    return pltpu.CompilerParams(vmem_limit_bytes=mebibytes * 2**20)


def in_hbm(array):
    return pltpu.with_memory_space_constraint(array, pltpu.HBM)


def dot(a, b):
    return jnp.dot(a, b, preferred_element_type=F32)


def silu(v):
    half = 0.5 * v
    return half + half * jnp.tanh(half)


def norm(value, gain):
    mean = jnp.mean(value, axis=-1, keepdims=True)
    centred = value - mean
    variance = jnp.mean(centred * centred, axis=-1, keepdims=True)
    return centred * lax.rsqrt(variance + 1e-05) * gain


def put_rows(table, start, value):
    rows, width = value.shape
    parts = width // 128
    for part in range(parts):
        table[pl.ds(start * parts + part, rows, stride=parts), :] = value[
            :, part * 128 : part * 128 + 128
        ]


def get_rows(table, start, rows, parts):
    return jnp.concatenate(
        [table[pl.ds(start * parts + part, rows, stride=parts), :] for part in range(parts)],
        axis=1,
    )


def slot_index(index, start, inner, scale):
    cap = index.shape[0]
    peer = start // cap + inner // cap
    return pl.multiple_of(index[inner % cap, peer] * scale, scale)


def pick_rows(at, table, target, base, rows, parts):
    for inner in range(rows):
        target[pl.ds(base * parts + inner * parts, parts), :] = table[pl.ds(at(inner), parts), :]


def pick_grid(index_in, grid_in, out, index, grid, table, picked, turned, index_sem, sems):
    features, rows = grid.shape
    slots = out.shape[0]
    step = STEP * 2

    def grid_copy(part):
        columns = pl.ds(pl.multiple_of(part * step, step), step)
        return pltpu.make_async_copy(grid_in.at[:, columns], grid.at[:, columns], sems.at[part])

    for part in range(rows // step):
        grid_copy(part).start()
    index_copy = pltpu.make_async_copy(index_in, index, index_sem)
    index_copy.start()

    @pl.loop(0, rows // STEP)
    def _(block):
        @pl.when(block % 2 == 0)
        def _():
            grid_copy(block // 2).wait()

        at = pl.multiple_of(block * STEP, STEP)
        turned[pl.ds(0, features), :] = grid[:, pl.ds(at, STEP)]
        put_rows(table, at, turned[...].T.astype(F32))

    index_copy.wait()
    step = 64

    @pl.loop(0, slots // step)
    def _(block):
        at = pl.multiple_of(block * step, step)
        pick_rows(lambda inner: slot_index(index, at, inner, 2), table, picked, at, step, 2)
        out[pl.ds(at, step), :] = get_rows(picked, at, step, 2)[:, :features].astype(BF16)


def piece(ref, part, rows):
    return ref.at[pl.ds(pl.multiple_of(part * rows, rows), rows)]


def mesh_side(
    dst, halo, mesh, enc_w, node_w,
    term_out, own_out, halo_out, folded_out,
    table, copies, picked, picked_too, own, terms, halves, latents, w_enc, w_node, sems,
):
    rows = mesh.shape[0]
    slots = halo_out.shape[0]
    step = 512
    chunks = rows // step
    weights = [
        pltpu.make_async_copy(enc_w.at[pl.ds(1, 2)], w_enc, sems.at[0]),
        pltpu.make_async_copy(node_w.at[pl.ds(0, 2)], w_node, sems.at[1]),
    ]
    for copy in weights:
        copy.start()

    def latent_copy(part):
        return pltpu.make_async_copy(
            piece(mesh, part, step), piece(latents, part, step), sems.at[2 + part]
        )

    for part in range(chunks):
        latent_copy(part).start()
    for copy in weights:
        copy.wait()

    @pl.loop(0, chunks)
    def _(block):
        at = pl.multiple_of(block * step, step)
        latent_copy(block).wait()
        value = latents[pl.ds(at, step), :]
        put_rows(table, at, dot(value, w_enc[0]))
        put_rows(own, at, dot(value, w_node[0]))
        put_rows(copies, at, value.astype(F32))

    outs = [pltpu.make_async_copy(own, own_out, sems.at[0])]
    outs[0].start()
    folded_out[...] = dot(w_enc[1], w_node[1]).astype(BF16)
    step = 64
    parts = 4
    span = slots // parts
    for part in range(parts):

        @pl.loop(part * span // step, (part + 1) * span // step)
        def _(block):
            at = pl.multiple_of(block * step, step)
            pick_rows(lambda inner: slot_index(dst, at, inner, 4), table, picked_too, at, step, 4)
            pick_rows(lambda inner: slot_index(halo, at, inner, 4), copies, picked, at, step, 4)
            terms[pl.ds(at, step), :] = get_rows(picked_too, at, step, 4).astype(BF16)
            halves[pl.ds(at, step), :] = get_rows(picked, at, step, 4).astype(BF16)

        outs.append(
            pltpu.make_async_copy(
                piece(terms, part, span), piece(term_out, part, span), sems.at[2 + part]
            )
        )
        outs[-1].start()
    outs.append(pltpu.make_async_copy(halves, halo_out, sems.at[1]))
    outs[-1].start()
    for copy in outs:
        copy.wait()


def node_update(pre, own, w_out, gain):
    return (own.astype(F32) + norm(dot(silu(pre).astype(BF16), w_out), gain)).astype(BF16)


def encode(
    target, halo, rows_in, mesh_term, own, own_halo, embed_in, embed_out, enc_w, folded, node_w,
    gains, sums_out, halo_out,
    sums, terms, first, second, halves, w_grid, w_message, w_out, halo_rows, sems,
):
    slots = rows_in.shape[0]
    mesh_rows = own.shape[0]
    blocks = slots // STEP
    copies = [
        pltpu.make_async_copy(enc_w.at[0], w_grid, sems.at[0]),
        pltpu.make_async_copy(folded, w_message, sems.at[1]),
        pltpu.make_async_copy(mesh_term, terms, sems.at[2]),
        pltpu.make_async_copy(own, sums.at[pl.ds(0, mesh_rows)], sems.at[3]),
        pltpu.make_async_copy(node_w.at[2], w_out, sems.at[4]),
        pltpu.make_async_copy(own_halo, halves, sems.at[5]),
    ]
    for copy in copies:
        copy.start()
    sums[pl.ds(mesh_rows, 8), :] = jnp.zeros((8, 128), F32)
    for copy in copies[:3]:
        copy.wait()

    def message(block, into):
        at = pl.multiple_of(block * STEP, STEP)
        hidden = silu(dot(rows_in[pl.ds(at, STEP), :], embed_in[...])).astype(BF16)
        latent = norm(dot(hidden, embed_out[...]), gains[0:1, :]).astype(BF16)
        pre = dot(latent, w_grid[...]) + terms[pl.ds(at, STEP), :].astype(F32)
        put_rows(into, 0, dot(silu(pre).astype(BF16), w_message[...]))

    def scatter(block, source):
        for inner in range(STEP):
            row = pl.ds(slot_index(target, block * STEP, inner, 4), 4)
            sums[row, :] = sums[row, :] + source[pl.ds(inner * 4, 4), :]

    message(0, first)
    copies[3].wait()

    @pl.loop(0, blocks // 2 - 1)
    def _(pair):
        message(pair * 2 + 1, second)
        scatter(pair * 2, first)
        message(pair * 2 + 2, first)
        scatter(pair * 2 + 1, second)

    message(blocks - 1, second)
    scatter(blocks - 2, first)
    scatter(blocks - 1, second)
    sums_copy = pltpu.make_async_copy(sums.at[pl.ds(0, mesh_rows)], sums_out, sems.at[3])
    sums_copy.start()
    for copy in copies[4:]:
        copy.wait()

    def pick(block, into):
        pick_rows(lambda inner: slot_index(halo, block * STEP, inner, 4), sums, into, 0, STEP, 4)

    def update(block, source):
        at = pl.multiple_of(block * STEP, STEP)
        halo_rows[pl.ds(at, STEP), :] = node_update(
            get_rows(source, 0, STEP, 4), halves[pl.ds(at, STEP), :], w_out[...], gains[1:2, :]
        )

    pick(0, first)

    def halo_copy(pair):
        return pltpu.make_async_copy(
            piece(halo_rows, pair, STEP * 2), piece(halo_out, pair, STEP * 2), sems.at[6 + pair]
        )

    @pl.loop(0, blocks // 2)
    def _(pair):
        pick(pair * 2 + 1, second)
        update(pair * 2, first)
        pick(jnp.minimum(pair * 2 + 2, blocks - 1), first)
        update(pair * 2 + 1, second)
        halo_copy(pair).start()

    sums_copy.wait()
    for pair in range(blocks // 2):
        halo_copy(pair).wait()


def local_terms(
    dst, src, sums_in, mesh, node_w, proc_w, gains, edges_in, mesh_out, out,
    sums, latents, edges, new, local, w_node, w_proc, receivers, senders, picked, sems, edge_sems,
):
    rows = mesh.shape[0]
    step = 512
    chunks = rows // step
    edge_chunks = edges.shape[0] // step
    weights = [
        pltpu.make_async_copy(node_w.at[2], w_node, sems.at[0]),
        pltpu.make_async_copy(proc_w.at[pl.ds(0, 3)], w_proc, sems.at[1]),
    ]

    def sums_copy(part):
        return pltpu.make_async_copy(
            piece(sums_in, part, step * 4), piece(sums, part, step * 4), sems.at[2 + part]
        )

    def latent_copy(part):
        return pltpu.make_async_copy(
            piece(mesh, part, step), piece(latents, part, step), sems.at[2 + chunks + part]
        )

    def new_copy(part):
        return pltpu.make_async_copy(
            piece(new, part, step), piece(mesh_out, part, step), sems.at[2 + part]
        )

    def edge_copy(part):
        return pltpu.make_async_copy(
            piece(edges_in, part, step), piece(edges, part, step), edge_sems.at[0, part]
        )

    def local_copy(part):
        return pltpu.make_async_copy(
            piece(local, part, step), piece(out, part, step), edge_sems.at[1, part]
        )

    for copy in weights:
        copy.start()
    for part in range(chunks):
        sums_copy(part).start()
        latent_copy(part).start()
    for part in range(edge_chunks):
        edge_copy(part).start()
    senders[pl.ds(rows * 4, 8), :] = jnp.zeros((8, 128), F32)
    for copy in weights:
        copy.wait()

    @pl.loop(0, chunks)
    def _(block):
        at = pl.multiple_of(block * step, step)
        sums_copy(block).wait()
        latent_copy(block).wait()
        value = node_update(
            get_rows(sums, at, step, 4), latents[pl.ds(at, step), :], w_node[...], gains[1:2, :]
        )
        new[pl.ds(at, step), :] = value
        put_rows(receivers, at, dot(value, w_proc[1]))
        put_rows(senders, at, dot(value, w_proc[2]))
        new_copy(block).start()

    @pl.loop(0, edge_chunks)
    def _(block):
        start = pl.multiple_of(block * step, step)
        edge_copy(block).wait()

        @pl.loop(0, step // 32)
        def _(group):
            for inner in range(32):
                row = group * 32 + inner
                one = pl.multiple_of(dst[start + row], 4)
                two = pl.multiple_of(src[start + row], 4)
                picked[pl.ds(pl.multiple_of(row * 4, 4), 4), :] = (
                    receivers[pl.ds(one, 4), :] + senders[pl.ds(two, 4), :]
                )

        here = pl.ds(start, step)
        value = dot(edges[here, :], w_proc[0]) + get_rows(picked, 0, step, 4)
        local[here, :] = value.astype(BF16)
        local_copy(block).start()

    for part in range(chunks):
        new_copy(part).wait()
    for part in range(edge_chunks):
        local_copy(part).wait()


def edge_update(
    src, halo, proc_w, edges_in, local_in, gains, out,
    w_proc, edges, local, new, senders, first, second, sems, edge_sems,
):
    rows = halo.shape[0]
    step = 512
    chunks = rows // step
    edge_chunks = edges.shape[0] // step
    last = src.shape[0] // STEP - 1
    weights = pltpu.make_async_copy(proc_w.at[pl.ds(2, 2)], w_proc, sems.at[0])

    def edge_copy(part):
        return pltpu.make_async_copy(
            piece(edges_in, part, step), piece(edges, part, step), edge_sems.at[0, part]
        )

    def local_copy(part):
        return pltpu.make_async_copy(
            piece(local_in, part, step), piece(local, part, step), edge_sems.at[1, part]
        )

    def new_copy(part):
        return pltpu.make_async_copy(
            piece(new, part, step), piece(out, part, step), edge_sems.at[0, part]
        )

    weights.start()
    for part in range(edge_chunks):
        local_copy(part).start()
        edge_copy(part).start()
    senders[pl.ds(rows * 4, 8), :] = jnp.zeros((8, 128), F32)
    weights.wait()

    @pl.loop(0, chunks)
    def _(block):
        at = pl.multiple_of(block * step, step)
        put_rows(senders, at, dot(halo[pl.ds(at, step), :], w_proc[0]))

    def pick(block, into):
        at = block * STEP
        pick_rows(lambda inner: pl.multiple_of(src[at + inner], 4), senders, into, 0, STEP, 4)

    def update(block, source):
        here = pl.ds(pl.multiple_of(block * STEP, STEP), STEP)
        hidden = silu(local[here, :].astype(F32) + get_rows(source, 0, STEP, 4)).astype(BF16)
        change = norm(dot(hidden, w_proc[1]), gains[2:3, :])
        new[here, :] = (edges[here, :].astype(F32) + change).astype(BF16)

    pick(0, first)

    @pl.loop(0, edge_chunks)
    def _(pair):
        edge_copy(pair).wait()
        local_copy(pair).wait()
        pick(pair * 2 + 1, second)
        update(pair * 2, first)
        pick(jnp.minimum(pair * 2 + 2, last), first)
        update(pair * 2 + 1, second)
        new_copy(pair).start()

    for part in range(edge_chunks):
        new_copy(part).wait()


def shards(
    grid_in,
    embed_in,
    embed_out,
    mesh_latent,
    edge_latent,
    enc_w,
    node_w,
    proc_w,
    gains,
    g2m_src,
    g2m_dst,
    g2m_count,
    halo_rows,
    proc_dst,
    proc_src,
):
    axes = ("band", "tile")
    peers = lax.axis_size("band") * lax.axis_size("tile")
    grid_rows, features = grid_in.shape
    mesh_rows, width = mesh_latent.shape
    edges = edge_latent.shape[0]
    cap = g2m_src.shape[2]
    halo_cap = halo_rows.shape[2]
    slots = peers * cap
    halo_slots = peers * halo_cap
    parts = width // 128

    def full(rows, columns, dtype):
        return jax.ShapeDtypeStruct((rows, columns), dtype)

    def scratch(rows, columns=128, dtype=F32):
        return pltpu.VMEM((rows, columns), dtype)

    def cost(flops, moved):
        return pl.CostEstimate(flops=flops, bytes_accessed=moved, transcendentals=0)

    def sems(*counts):
        return pltpu.SemaphoreType.DMA(counts)

    outgoing = pl.pallas_call(
        pick_grid,
        out_shape=full(slots, features, BF16),
        in_specs=[ANY, ANY],
        out_specs=VMEM,
        scratch_shapes=[
            pltpu.SMEM((cap, peers), jnp.int32),
            scratch(features, grid_rows, BF16),
            scratch(grid_rows * 2),
            scratch(slots * 2),
            scratch(256, STEP, BF16),
            pltpu.SemaphoreType.DMA,
            sems(grid_rows // (STEP * 2)),
        ],
        compiler_params=params(14),
        name="pick_grid",
    )(in_hbm(g2m_src[0].T), in_hbm(grid_in.T))
    arrived = lax.all_to_all(
        outgoing.reshape(peers, cap, features), axes, split_axis=0, concat_axis=0, tiled=True
    ).reshape(slots, features)

    dst = g2m_dst[0].T
    halo = halo_rows[0].T
    mesh_term, own, own_halo, folded = pl.pallas_call(
        mesh_side,
        out_shape=(
            pltpu.HBM((slots, width), BF16),
            pltpu.HBM((mesh_rows * parts, 128), F32),
            pltpu.HBM((halo_slots, width), BF16),
            full(width, width, BF16),
        ),
        in_specs=[SMEM, SMEM, ANY, ANY, ANY],
        out_specs=(ANY, ANY, ANY, VMEM),
        scratch_shapes=[
            scratch(mesh_rows * parts),
            scratch(mesh_rows * parts),
            scratch(halo_slots * parts),
            scratch(slots * parts),
            scratch(mesh_rows * parts),
            scratch(slots, width, BF16),
            scratch(halo_slots, width, BF16),
            scratch(mesh_rows, width, BF16),
            pltpu.VMEM((2, width, width), BF16),
            pltpu.VMEM((2, width, width), BF16),
            sems(2 + mesh_rows // 512),
        ],
        compiler_params=params(40),
        cost_estimate=cost(10**10, 2 * 10**7),
        name="mesh_side",
    )(dst, halo, in_hbm(mesh_latent), in_hbm(enc_w), in_hbm(node_w))

    live = jnp.arange(cap, dtype=jnp.int32)[:, None] < g2m_count
    sums, halo_out = pl.pallas_call(
        encode,
        out_shape=(
            pltpu.HBM((mesh_rows * parts, 128), F32),
            pltpu.HBM((halo_slots, width), BF16),
        ),
        in_specs=[SMEM, SMEM, VMEM, ANY, ANY, ANY, VMEM, VMEM, ANY, ANY, ANY, VMEM],
        out_specs=(ANY, ANY),
        scratch_shapes=[
            scratch(mesh_rows * parts + 8),
            scratch(slots, width, BF16),
            scratch(STEP * parts),
            scratch(STEP * parts),
            scratch(halo_slots, width, BF16),
            scratch(width, width, BF16),
            scratch(width, width, BF16),
            scratch(width, width, BF16),
            scratch(halo_slots, width, BF16),
            sems(6 + halo_slots // STEP // 2),
        ],
        compiler_params=params(24),
        name="encode",
    )(
        jnp.where(live, dst, mesh_rows), halo, arrived, in_hbm(mesh_term), in_hbm(own),
        in_hbm(own_halo), embed_in, embed_out, in_hbm(enc_w), folded, in_hbm(node_w), gains,
    )
    halo_in = lax.all_to_all(
        halo_out.reshape(peers, halo_cap, width), axes, split_axis=0, concat_axis=0, tiled=True
    ).reshape(halo_slots, width)

    remote = proc_src >= mesh_rows
    mesh_new, local = pl.pallas_call(
        local_terms,
        out_shape=(pltpu.HBM((mesh_rows, width), BF16), pltpu.HBM((edges, width), BF16)),
        in_specs=[SMEM, SMEM, ANY, ANY, ANY, ANY, VMEM, ANY],
        out_specs=(ANY, ANY),
        scratch_shapes=[
            scratch(mesh_rows * parts),
            scratch(mesh_rows, width, BF16),
            scratch(edges, width, BF16),
            scratch(mesh_rows, width, BF16),
            scratch(edges, width, BF16),
            scratch(width, width, BF16),
            pltpu.VMEM((3, width, width), BF16),
            scratch(mesh_rows * parts),
            scratch(mesh_rows * parts + 8),
            scratch(512 * parts),
            sems(2 + 2 * (mesh_rows // 512)),
            sems(2, edges // 512),
        ],
        compiler_params=params(40),
        cost_estimate=cost(2 * 10**10, 4 * 10**7),
        name="local_terms",
    )(
        proc_dst * parts,
        jnp.where(remote, mesh_rows, proc_src) * parts,
        in_hbm(sums),
        in_hbm(mesh_latent),
        in_hbm(node_w),
        in_hbm(proc_w),
        gains,
        in_hbm(edge_latent),
    )
    edge_new = pl.pallas_call(
        edge_update,
        out_shape=pltpu.HBM((edges, width), BF16),
        in_specs=[SMEM, VMEM, ANY, ANY, ANY, VMEM],
        out_specs=ANY,
        scratch_shapes=[
            pltpu.VMEM((2, width, width), BF16),
            scratch(edges, width, BF16),
            scratch(edges, width, BF16),
            scratch(edges, width, BF16),
            scratch(halo_slots * parts + 8),
            scratch(STEP * parts),
            scratch(STEP * parts),
            sems(1),
            sems(2, edges // 512),
        ],
        compiler_params=params(28),
        name="edge_update",
    )(
        jnp.where(remote, proc_src - mesh_rows, halo_slots) * parts,
        halo_in,
        in_hbm(proc_w),
        in_hbm(edge_latent),
        in_hbm(local),
        gains,
    )
    return (mesh_new, edge_new)


def solution(mesh):
    rows = P(("band", "tile"), None)
    slots = P(("band", "tile"), None, None)
    flat = P(("band", "tile"))
    in_specs = (
        rows, P(), P(), rows, rows, P(), P(), P(), P(), slots, slots, rows, slots, flat, flat,
    )
    return jax.shard_map(
        shards, mesh=mesh, in_specs=in_specs, out_specs=(rows, rows), check_vma=False
    )
```

time: 125 us -> 110 us (0.88)
  local copies, waits for them, and re-layouts: 6.13 us -> 0.04 us
  Pallas kernels: 84 us -> 78.8 us
  waiting for transfers between devices: 15 us -> 12.9 us
    pallas_call x4, Pallas kernels: 78.3 us -> 72.1 us  [the longest x1 21.5 us: shards(): pl.pallas_call(encode, out_shape=(pltpu.HBM((mesh_rows * parts, 128), F32...]
    unnamed x18 -> x16, local copies, waits for them, and re-layouts: 4.12 us -> 0.04 us
    all_to_all x1, waiting for transfers between devices: 10.3 us -> 8.35 us  [shards(): lax.all_to_all(halo_out.reshape(peers, halo_cap, width), axes, split_axis...]
    squeeze x1 -> x0, local copies, waits for them, and re-layouts: 1.27 us -> none  [shards(): node_w[0]]
  transfers between devices with their start and end apart: 2 -> 2, of which waited for: 2 -> 2; matrix products, arithmetic and copies ran while one was open for 2% -> 0% of each run, Pallas kernels for 25% -> 32%
where the time goes in v2:
time: 110 us
  Pallas kernels  78.8 us (72%)
  starting transfers between devices  16.7 us (15%)
  waiting for transfers between devices  12.9 us (12%)
    pallas_call x1, Pallas kernels, shards(): pl.pallas_call(encode, out_shape=(pltpu.HBM((mesh_rows * parts, 128), F32...  21.5 us
    pallas_call x1, Pallas kernels, shards(): pl.pallas_call(local_terms, out_shape=(pltpu.HBM((mesh_rows, width), BF16...  21.3 us
    pallas_call x1, Pallas kernels, shards(): pl.pallas_call(edge_update, out_shape=pltpu.HBM((edges, width), BF16), in...  15.3 us
    pallas_call x1, Pallas kernels, shards(): pl.pallas_call(mesh_side, out_shape=(pltpu.HBM((slots, width), BF16), plt...  13.9 us
    all_to_all x1, starting transfers between devices, shards(): lax.all_to_all(outgoing.reshape(peers, cap, features), axes, split_axis=0...  11.5 us
    all_to_all x1, waiting for transfers between devices, shards(): lax.all_to_all(halo_out.reshape(peers, halo_cap, width), axes, split_axis...  8.35 us
    pallas_call x1, Pallas kernels, shards(): pl.pallas_call(pick_grid, out_shape=full(slots, features, BF16), in_specs...  6.75 us
    all_to_all x1, starting transfers between devices, shards(): lax.all_to_all(halo_out.reshape(peers, halo_cap, width), axes, split_axis...  5.23 us
  transfers between devices with their start and end apart: 2, of which 2 were waited for; matrix products, arithmetic and copies ran while one was open for 0% of the time, Pallas kernels for 32%

profile of v2, /device:TPU:1, one launch (start us, length us, event | category | flops | bytes accessed | tf_op | source)
XLA Modules:
  0.0 109.5 jit_solution(17891266082560790051)
XLA Ops:
  0.6 0.0 copy-start.5
  0.6 0.0 copy-start.4
  0.7 0.0 copy-start.7
  0.7 0.0 copy-start.3
  0.7 6.7 %pick_grid.1 = bf16[2048,227]{1,0:T(8,128)(2,1)} custom-call(s32[16,128]{1,0:T(8,128)} %bitcast.23, bf16[227,4096]{1,0:T(8,128)(2,1)} %bitcast.22), custom_call_target="tpu_custom_call" | custom-call | tf_op jit(solution)/shard_map/pick_grid/pallas_call | solution.py:445
  7.4 11.5 %all-to-all-start = ((bf16[128,16,227]{2,1,0:T(8,128)(2,1)}), bf16[128,16,227]{2,1,0:T(8,128)(2,1)S(1)}, u32[]{:S(2)}, u32[]{:S(2)}) async-start(bf16[128,16,227]{2,1,0:T(8,128)(2,1)} %bitcast.8), calls=%async_computation | async-start | bytes 2097152 | tf_op jit(solution)/shard_map/all_to_all | solution.py:462
  18.9 0.0 copy-done.5
  19.0 0.0 copy-done.4
  19.0 0.0 copy-done.7
  19.0 0.0 copy-done.3
  19.0 0.0 copy-start
  19.0 0.0 copy-start.1
  19.0 0.0 copy-start.2
  19.0 13.9 %mesh_side.1 = (bf16[2048,512]{1,0:T(8,128)(2,1)}, f32[10240,128]{1,0:T(8,128)}, bf16[2048,512]{1,0:T(8,128)(2,1)}, bf16[512,512]{1,0:T(8,128)(2,1)S(1)}) custom-call(s32[16,128]{1,0:T(8,128)S(1)} %bitcast.20, s32[16,128]{1,0:T(8,128)S(1)} %bitcast.18, bf16[2560,512]{1,0:T(8,128)(2,1)} %mesh.3, bf16[3,512,512]{2,1,0:T(8,128)(2,1)} %enc_w.3, ...), custom_call_target="tpu_custom_call" | custom-call | flops 10000000000 | bytes 20000000 | tf_op jit(solution)/shard_map/mesh_side/pallas_call | solution.py:468
  33.0 4.6 %all-to-all-done = bf16[128,16,227]{2,1,0:T(8,128)(2,1)S(1)} async-done(((bf16[128,16,227]{2,1,0:T(8,128)(2,1)}), bf16[128,16,227]{2,1,0:T(8,128)(2,1)S(1)}, u32[]{:S(2)}, u32[]{:S(2)}) %all-to-all-start) | async-done | bytes 929824 | tf_op jit(solution)/shard_map/all_to_all | solution.py:462
  37.6 0.0 copy-done
  37.6 0.0 copy-done.1
  37.6 0.0 copy-done.2
  37.6 21.5 %encode.1 = (f32[10240,128]{1,0:T(8,128)}, bf16[2048,512]{1,0:T(8,128)(2,1)}) custom-call(s32[16,128]{1,0:T(8,128)S(1)} %fusion.2.target, s32[16,128]{1,0:T(8,128)S(1)} %bitcast.19, bf16[2048,227]{1,0:T(8,128)(2,1)S(1)} %bitcast.17, bf16[2048,512]{1,0:T(8,128)(2,1)} %get-tuple-element.10.mesh_term, f32[10240,128]{1,0:T(8,128)} %get-tuple-element.11.own, ...), custom_call_target="tpu_custom_call" | custom-call | tf_op jit(solution)/shard_map/encode/pallas_call | solution.py:497
  59.1 0.0 copy-start.6
  59.1 5.2 %all-to-all-start.1 = ((bf16[128,16,512]{2,1,0:T(8,128)(2,1)}), bf16[128,16,512]{2,1,0:T(8,128)(2,1)S(1)}, u32[]{:S(2)}, u32[]{:S(2)}) async-start(bf16[128,16,512]{2,1,0:T(8,128)(2,1)} %bitcast.21), calls=%async_computation.1 | async-start | bytes 4194304 | tf_op jit(solution)/shard_map/all_to_all | solution.py:523
  64.4 0.0 copy-done.6
  64.4 21.3 %local_terms.1 = (bf16[2560,512]{1,0:T(8,128)(2,1)}, bf16[4096,512]{1,0:T(8,128)(2,1)}) custom-call(s32[4096]{0:T(1024)S(1)} %broadcast_multiply_fusion.dst, s32[4096]{0:T(1024)S(1)} %get-tuple-element.19.src, f32[10240,128]{1,0:T(8,128)} %get-tuple-element.14.sums_in, bf16[2560,512]{1,0:T(8,128)(2,1)} %mesh.3, bf16[3,512,512]{2,1,0:T(8,128)(2,1)} %node_w.5, ...), custom_call_target="tpu_custom_call" | custom-call | flops 20000000000 | bytes 40000000 | tf_op jit(solution)/shard_map/local_terms/pallas_call | solution.py:528
  85.6 8.3 %all-to-all-done.1 = bf16[128,16,512]{2,1,0:T(8,128)(2,1)S(1)} async-done(((bf16[128,16,512]{2,1,0:T(8,128)(2,1)}), bf16[128,16,512]{2,1,0:T(8,128)(2,1)S(1)}, u32[]{:S(2)}, u32[]{:S(2)}) %all-to-all-start.1) | async-done | bytes 2097184 | tf_op jit(solution)/shard_map/all_to_all | solution.py:523
  94.0 15.3 %edge_update.1 = bf16[4096,512]{1,0:T(8,128)(2,1)} custom-call(s32[4096]{0:T(1024)S(1)} %get-tuple-element.18.src, bf16[2048,512]{1,0:T(8,128)(2,1)S(1)} %bitcast.16, bf16[4,512,512]{2,1,0:T(8,128)(2,1)} %proc_w.3, bf16[4096,512]{1,0:T(8,128)(2,1)} %edges_in.3, bf16[4096,512]{1,0:T(8,128)(2,1)} %get-tuple-element.17.local_in, f32[3,512]{1,0:T(4,128)S(1)} %copy-done.2), custom_call_target="tpu_custom_call" | custom-call | tf_op jit(solution)/shard_map/edge_update/pallas_call | solution.py:560
  (3 shorter events, 0.0 us)
Async XLA Ops:
  0.6 18.3 %copy-start.5 = (s32[4096]{0:T(1024)S(1)}, s32[4096]{0:T(1024)}, u32[]{:S(2)}) copy-start(s32[4096]{0:T(1024)} %param.29) | copy-start | bytes 49156
  0.6 18.3 %copy-start.4 = (s32[1,128,16]{1,2,0:T(8,128)S(1)}, s32[1,128,16]{1,2,0:T(8,128)}, u32[]{:S(2)}) copy-start(s32[1,128,16]{1,2,0:T(8,128)} %param.25) | copy-start | bytes 24580
  0.7 18.3 %copy-start.7 = (s32[1,128]{1,0:T(1,128)S(1)}, s32[1,128]{1,0:T(1,128)}, u32[]{:S(2)}) copy-start(s32[1,128]{1,0:T(1,128)} %param.26) | copy-start | bytes 1540
  0.7 18.3 %copy-start.3 = (s32[1,128,16]{1,2,0:T(8,128)S(1)}, s32[1,128,16]{1,2,0:T(8,128)}, u32[]{:S(2)}) copy-start(s32[1,128,16]{1,2,0:T(8,128)} %param.27) | copy-start | bytes 24580
  7.4 30.1 %all-to-all-start = ((bf16[128,16,227]{2,1,0:T(8,128)(2,1)}), bf16[128,16,227]{2,1,0:T(8,128)(2,1)S(1)}, u32[]{:S(2)}, u32[]{:S(2)}) async-start(bf16[128,16,227]{2,1,0:T(8,128)(2,1)} %bitcast.8), calls=%async_computation | async-start | bytes 2097152 | tf_op jit(solution)/shard_map/all_to_all | solution.py:462
  19.0 18.6 %copy-start = (bf16[512,512]{1,0:T(8,128)(2,1)S(1)}, bf16[512,512]{1,0:T(8,128)(2,1)}, u32[]{:S(2)}) copy-start(bf16[512,512]{1,0:T(8,128)(2,1)} %embed_out.1) | copy-start | bytes 1572868
  19.0 18.5 %copy-start.1 = (bf16[227,512]{1,0:T(8,128)(2,1)S(1)}, bf16[227,512]{1,0:T(8,128)(2,1)}, u32[]{:S(2)}) copy-start(bf16[227,512]{1,0:T(8,128)(2,1)} %embed_in.1) | copy-start | bytes 697348
  19.0 18.5 %copy-start.2 = (f32[3,512]{1,0:T(4,128)S(1)}, f32[3,512]{1,0:T(4,128)}, u32[]{:S(2)}) copy-start(f32[3,512]{1,0:T(4,128)} %gains.5) | copy-start | bytes 18436
  59.1 5.2 %copy-start.6 = (s32[4096]{0:T(1024)S(1)}, s32[4096]{0:T(1024)}, u32[]{:S(2)}) copy-start(s32[4096]{0:T(1024)} %param.28) | copy-start | bytes 49156
  59.1 34.9 %all-to-all-start.1 = ((bf16[128,16,512]{2,1,0:T(8,128)(2,1)}), bf16[128,16,512]{2,1,0:T(8,128)(2,1)S(1)}, u32[]{:S(2)}, u32[]{:S(2)}) async-start(bf16[128,16,512]{2,1,0:T(8,128)(2,1)} %bitcast.21), calls=%async_computation.1 | async-start | bytes 4194304 | tf_op jit(solution)/shard_map/all_to_all | solution.py:523

commit v3 on v2

--- a/solution.py
+++ b/solution.py
@@ -11,6 +11,9 @@
 SMEM = pl.BlockSpec(memory_space=pltpu.SMEM)
 ANY = pl.BlockSpec(memory_space=pl.ANY)
 STEP = 256
+MESSAGE_STEP = 1024
+HALO_STEP = 512
+EDGE_STEP = 512
 
 
 def params(mebibytes):
@@ -53,10 +56,9 @@
     )
 
 
-def slot_index(index, start, inner, scale):
+def slot_index(index, peer, inner, scale):
     cap = index.shape[0]
-    peer = start // cap + inner // cap
-    return pl.multiple_of(index[inner % cap, peer] * scale, scale)
+    return pl.multiple_of(index[inner % cap, peer + inner // cap] * scale, scale)
 
 
 def pick_rows(at, table, target, base, rows, parts):
@@ -64,7 +66,9 @@
         target[pl.ds(base * parts + inner * parts, parts), :] = table[pl.ds(at(inner), parts), :]
 
 
-def pick_grid(index_in, grid_in, out, index, grid, table, picked, turned, index_sem, sems):
+def pick_grid(
+    index_in, grid_in, out_hbm, index, grid, table, picked, turned, out, index_sem, sems, out_sems
+):
     features, rows = grid.shape
     slots = out.shape[0]
     step = STEP * 2
@@ -89,13 +93,27 @@
         put_rows(table, at, turned[...].T.astype(F32))
 
     index_copy.wait()
-    step = 64
-
-    @pl.loop(0, slots // step)
-    def _(block):
-        at = pl.multiple_of(block * step, step)
-        pick_rows(lambda inner: slot_index(index, at, inner, 2), table, picked, at, step, 2)
-        out[pl.ds(at, step), :] = get_rows(picked, at, step, 2)[:, :features].astype(BF16)
+    step = 128
+    span = slots // out_sems.shape[0]
+
+    def out_copy(part):
+        return pltpu.make_async_copy(
+            piece(out, part, span), piece(out_hbm, part, span), out_sems.at[part]
+        )
+
+    for part in range(slots // span):
+
+        @pl.loop(part * span // step, (part + 1) * span // step)
+        def _(block):
+            at = pl.multiple_of(block * step, step)
+            first = block * (step // index.shape[0])
+            pick_rows(lambda inner: slot_index(index, first, inner, 2), table, picked, at, step, 2)
+            out[pl.ds(at, step), :] = get_rows(picked, at, step, 2)[:, :features].astype(BF16)
+
+        out_copy(part).start()
+
+    for part in range(slots // span):
+        out_copy(part).wait()
 
 
 def piece(ref, part, rows):
@@ -148,8 +166,8 @@
         @pl.loop(part * span // step, (part + 1) * span // step)
         def _(block):
             at = pl.multiple_of(block * step, step)
-            pick_rows(lambda inner: slot_index(dst, at, inner, 4), table, picked_too, at, step, 4)
-            pick_rows(lambda inner: slot_index(halo, at, inner, 4), copies, picked, at, step, 4)
+            pick_rows(lambda inner: slot_index(dst, block * (step // dst.shape[0]), inner, 4), table, picked_too, at, step, 4)
+            pick_rows(lambda inner: slot_index(halo, block * (step // halo.shape[0]), inner, 4), copies, picked, at, step, 4)
             terms[pl.ds(at, step), :] = get_rows(picked_too, at, step, 4).astype(BF16)
             halves[pl.ds(at, step), :] = get_rows(picked, at, step, 4).astype(BF16)
 
@@ -172,11 +190,11 @@
 def encode(
     target, halo, rows_in, mesh_term, own, own_halo, embed_in, embed_out, enc_w, folded, node_w,
     gains, sums_out, halo_out,
-    sums, terms, first, second, halves, w_grid, w_message, w_out, halo_rows, sems,
+    sums, terms, sent, first, second, halves, w_grid, w_message, w_out, halo_rows, sems,
 ):
     slots = rows_in.shape[0]
     mesh_rows = own.shape[0]
-    blocks = slots // STEP
+    blocks = slots // HALO_STEP
     copies = [
         pltpu.make_async_copy(enc_w.at[0], w_grid, sems.at[0]),
         pltpu.make_async_copy(folded, w_message, sems.at[1]),
@@ -190,51 +208,47 @@
     sums[pl.ds(mesh_rows, 8), :] = jnp.zeros((8, 128), F32)
     for copy in copies[:3]:
         copy.wait()
-
-    def message(block, into):
-        at = pl.multiple_of(block * STEP, STEP)
-        hidden = silu(dot(rows_in[pl.ds(at, STEP), :], embed_in[...])).astype(BF16)
+    step = MESSAGE_STEP
+
+    @pl.loop(0, slots // step)
+    def _(block):
+        at = pl.multiple_of(block * step, step)
+        hidden = silu(dot(rows_in[pl.ds(at, step), :], embed_in[...])).astype(BF16)
         latent = norm(dot(hidden, embed_out[...]), gains[0:1, :]).astype(BF16)
-        pre = dot(latent, w_grid[...]) + terms[pl.ds(at, STEP), :].astype(F32)
-        put_rows(into, 0, dot(silu(pre).astype(BF16), w_message[...]))
-
-    def scatter(block, source):
-        for inner in range(STEP):
-            row = pl.ds(slot_index(target, block * STEP, inner, 4), 4)
-            sums[row, :] = sums[row, :] + source[pl.ds(inner * 4, 4), :]
-
-    message(0, first)
+        pre = dot(latent, w_grid[...]) + terms[pl.ds(at, step), :].astype(F32)
+        put_rows(sent, at, dot(silu(pre).astype(BF16), w_message[...]))
+
     copies[3].wait()
 
-    @pl.loop(0, blocks // 2 - 1)
-    def _(pair):
-        message(pair * 2 + 1, second)
-        scatter(pair * 2, first)
-        message(pair * 2 + 2, first)
-        scatter(pair * 2 + 1, second)
-
-    message(blocks - 1, second)
-    scatter(blocks - 2, first)
-    scatter(blocks - 1, second)
+    @pl.loop(0, slots // 32)
+    def _(block):
+        for inner in range(32):
+            row = block * 32 + inner
+            to = pl.ds(pl.multiple_of(target[row], 4), 4)
+            sums[to, :] = sums[to, :] + sent[pl.ds(pl.multiple_of(row * 4, 4), 4), :]
+
     sums_copy = pltpu.make_async_copy(sums.at[pl.ds(0, mesh_rows)], sums_out, sems.at[3])
     sums_copy.start()
     for copy in copies[4:]:
         copy.wait()
 
     def pick(block, into):
-        pick_rows(lambda inner: slot_index(halo, block * STEP, inner, 4), sums, into, 0, STEP, 4)
+        at = block * HALO_STEP
+        pick_rows(
+            lambda inner: pl.multiple_of(halo[at + inner], 4), sums, into, 0, HALO_STEP, 4
+        )
 
     def update(block, source):
-        at = pl.multiple_of(block * STEP, STEP)
-        halo_rows[pl.ds(at, STEP), :] = node_update(
-            get_rows(source, 0, STEP, 4), halves[pl.ds(at, STEP), :], w_out[...], gains[1:2, :]
+        at = pl.multiple_of(block * HALO_STEP, HALO_STEP)
+        halo_rows[pl.ds(at, HALO_STEP), :] = node_update(
+            get_rows(source, 0, HALO_STEP, 4), halves[pl.ds(at, HALO_STEP), :], w_out[...], gains[1:2, :]
         )
 
     pick(0, first)
 
     def halo_copy(pair):
         return pltpu.make_async_copy(
-            piece(halo_rows, pair, STEP * 2), piece(halo_out, pair, STEP * 2), sems.at[6 + pair]
+            piece(halo_rows, pair, HALO_STEP * 2), piece(halo_out, pair, HALO_STEP * 2), sems.at[6 + pair]
         )
 
     @pl.loop(0, blocks // 2)
@@ -345,23 +359,24 @@
     rows = halo.shape[0]
     step = 512
     chunks = rows // step
-    edge_chunks = edges.shape[0] // step
-    last = src.shape[0] // STEP - 1
+    edge_step = EDGE_STEP * 2
+    edge_chunks = edges.shape[0] // edge_step
+    last = src.shape[0] // EDGE_STEP - 1
     weights = pltpu.make_async_copy(proc_w.at[pl.ds(2, 2)], w_proc, sems.at[0])
 
     def edge_copy(part):
         return pltpu.make_async_copy(
-            piece(edges_in, part, step), piece(edges, part, step), edge_sems.at[0, part]
+            piece(edges_in, part, edge_step), piece(edges, part, edge_step), edge_sems.at[0, part]
         )
 
     def local_copy(part):
         return pltpu.make_async_copy(
-            piece(local_in, part, step), piece(local, part, step), edge_sems.at[1, part]
+            piece(local_in, part, edge_step), piece(local, part, edge_step), edge_sems.at[1, part]
         )
 
     def new_copy(part):
         return pltpu.make_async_copy(
-            piece(new, part, step), piece(out, part, step), edge_sems.at[0, part]
+            piece(new, part, edge_step), piece(out, part, edge_step), edge_sems.at[0, part]
         )
 
     weights.start()
@@ -377,12 +392,12 @@
         put_rows(senders, at, dot(halo[pl.ds(at, step), :], w_proc[0]))
 
     def pick(block, into):
-        at = block * STEP
-        pick_rows(lambda inner: pl.multiple_of(src[at + inner], 4), senders, into, 0, STEP, 4)
+        at = block * EDGE_STEP
+        pick_rows(lambda inner: pl.multiple_of(src[at + inner], 4), senders, into, 0, EDGE_STEP, 4)
 
     def update(block, source):
-        here = pl.ds(pl.multiple_of(block * STEP, STEP), STEP)
-        hidden = silu(local[here, :].astype(F32) + get_rows(source, 0, STEP, 4)).astype(BF16)
+        here = pl.ds(pl.multiple_of(block * EDGE_STEP, EDGE_STEP), EDGE_STEP)
+        hidden = silu(local[here, :].astype(F32) + get_rows(source, 0, EDGE_STEP, 4)).astype(BF16)
         change = norm(dot(hidden, w_proc[1]), gains[2:3, :])
         new[here, :] = (edges[here, :].astype(F32) + change).astype(BF16)
 
@@ -444,17 +459,19 @@
 
     outgoing = pl.pallas_call(
         pick_grid,
-        out_shape=full(slots, features, BF16),
+        out_shape=pltpu.HBM((slots, features), BF16),
         in_specs=[ANY, ANY],
-        out_specs=VMEM,
+        out_specs=ANY,
         scratch_shapes=[
             pltpu.SMEM((cap, peers), jnp.int32),
             scratch(features, grid_rows, BF16),
             scratch(grid_rows * 2),
             scratch(slots * 2),
             scratch(256, STEP, BF16),
+            scratch(slots, features, BF16),
             pltpu.SemaphoreType.DMA,
             sems(grid_rows // (STEP * 2)),
+            sems(4),
         ],
         compiler_params=params(14),
         name="pick_grid",
@@ -505,19 +522,20 @@
         scratch_shapes=[
             scratch(mesh_rows * parts + 8),
             scratch(slots, width, BF16),
-            scratch(STEP * parts),
-            scratch(STEP * parts),
+            scratch(slots * parts),
+            scratch(HALO_STEP * parts),
+            scratch(HALO_STEP * parts),
             scratch(halo_slots, width, BF16),
             scratch(width, width, BF16),
             scratch(width, width, BF16),
             scratch(width, width, BF16),
             scratch(halo_slots, width, BF16),
-            sems(6 + halo_slots // STEP // 2),
+            sems(6 + halo_slots // HALO_STEP // 2),
         ],
-        compiler_params=params(24),
+        compiler_params=params(32),
         name="encode",
     )(
-        jnp.where(live, dst, mesh_rows), halo, arrived, in_hbm(mesh_term), in_hbm(own),
+        jnp.where(live, dst, mesh_rows).T.reshape(-1) * parts, halo.T.reshape(-1) * parts, arrived, in_hbm(mesh_term), in_hbm(own),
         in_hbm(own_halo), embed_in, embed_out, in_hbm(enc_w), folded, in_hbm(node_w), gains,
     )
     halo_in = lax.all_to_all(
@@ -568,10 +586,10 @@
             scratch(edges, width, BF16),
             scratch(edges, width, BF16),
             scratch(halo_slots * parts + 8),
-            scratch(STEP * parts),
-            scratch(STEP * parts),
+            scratch(EDGE_STEP * parts),
+            scratch(EDGE_STEP * parts),
             sems(1),
-            sems(2, edges // 512),
+            sems(2, edges // EDGE_STEP // 2),
         ],
         compiler_params=params(28),
         name="edge_update",

time: 110 us -> 108 us (0.982)
  Pallas kernels: 78.8 us -> 76.5 us
  transfers between devices with their start and end apart: 2 -> 2, of which waited for: 2 -> 2; matrix products, arithmetic and copies ran while one was open for 0% -> 1% of each run, Pallas kernels for 32% -> 33%
where the time goes in v3:
time: 108 us
  Pallas kernels  76.5 us (71%)
  starting transfers between devices  17.1 us (16%)
  waiting for transfers between devices  12.6 us (12%)
    pallas_call x1, Pallas kernels, shards(): pl.pallas_call(local_terms, out_shape=(pltpu.HBM((mesh_rows, width), BF16...  21.3 us
    pallas_call x1, Pallas kernels, shards(): pl.pallas_call(encode, out_shape=(pltpu.HBM((mesh_rows * parts, 128), F32...  20.6 us
    pallas_call x1, Pallas kernels, shards(): pl.pallas_call(edge_update, out_shape=pltpu.HBM((edges, width), BF16), in...  14.6 us
    pallas_call x1, Pallas kernels, shards(): pl.pallas_call(mesh_side, out_shape=(pltpu.HBM((slots, width), BF16), plt...  13.8 us
    all_to_all x1, starting transfers between devices, shards(): lax.all_to_all(outgoing.reshape(peers, cap, features), axes, split_axis=0...  11.5 us
    all_to_all x1, waiting for transfers between devices, shards(): lax.all_to_all(halo_out.reshape(peers, halo_cap, width), axes, split_axis...  8.35 us
    pallas_call x1, Pallas kernels, shards(): pl.pallas_call(pick_grid, out_shape=pltpu.HBM((slots, features), BF16), i...  6.2 us
    all_to_all x1, starting transfers between devices, shards(): lax.all_to_all(halo_out.reshape(peers, halo_cap, width), axes, split_axis...  5.59 us
  transfers between devices with their start and end apart: 2, of which 2 were waited for; matrix products, arithmetic and copies ran while one was open for 1% of the time, Pallas kernels for 33%

profile of v3, /device:TPU:1, one launch (start us, length us, event | category | flops | bytes accessed | tf_op | source)
XLA Modules:
  0.0 107.7 jit_solution(17557155345912189343)
XLA Ops:
  0.6 0.0 copy-start.3
  0.6 0.0 copy-start.7
  0.7 0.0 copy-start.4
  0.7 0.0 copy-start.5
  0.7 6.2 %pick_grid.1 = bf16[2048,227]{1,0:T(8,128)(2,1)} custom-call(s32[16,128]{1,0:T(8,128)} %bitcast.22, bf16[227,4096]{1,0:T(8,128)(2,1)} %bitcast.21), custom_call_target="tpu_custom_call" | custom-call | tf_op jit(solution)/shard_map/pick_grid/pallas_call | solution.py:460
  6.9 11.5 %all-to-all-start = ((bf16[128,16,227]{2,1,0:T(8,128)(2,1)}), bf16[128,16,227]{2,1,0:T(8,128)(2,1)S(1)}, u32[]{:S(2)}, u32[]{:S(2)}) async-start(bf16[128,16,227]{2,1,0:T(8,128)(2,1)} %bitcast.19), calls=%async_computation | async-start | bytes 2097152 | tf_op jit(solution)/shard_map/all_to_all | solution.py:479
  18.4 0.0 copy-done.3
  18.4 0.1 copy.17
  18.5 0.1 squeeze.11
  18.6 0.0 copy-done.7
  18.6 0.1 iota_compare_fusion
  18.7 0.1 lt.24
  18.8 0.0 copy-done.4
  18.8 0.1 copy.18
  18.9 0.1 mul.21.halo
  19.0 0.0 copy-done.5
  19.0 0.0 copy-start
  19.0 0.0 copy-start.1
  19.0 0.0 copy-start.2
  19.0 13.8 %mesh_side.1 = (bf16[2048,512]{1,0:T(8,128)(2,1)}, f32[10240,128]{1,0:T(8,128)}, bf16[2048,512]{1,0:T(8,128)(2,1)}, bf16[512,512]{1,0:T(8,128)(2,1)S(1)}) custom-call(s32[16,128]{1,0:T(8,128)S(1)} %bitcast.17, s32[16,128]{1,0:T(8,128)S(1)} %bitcast.18, bf16[2560,512]{1,0:T(8,128)(2,1)} %mesh.3, bf16[3,512,512]{2,1,0:T(8,128)(2,1)} %enc_w.3, ...), custom_call_target="tpu_custom_call" | custom-call | flops 10000000000 | bytes 20000000 | tf_op jit(solution)/shard_map/mesh_side/pallas_call | solution.py:485
  32.8 4.2 %all-to-all-done = bf16[128,16,227]{2,1,0:T(8,128)(2,1)S(1)} async-done(((bf16[128,16,227]{2,1,0:T(8,128)(2,1)}), bf16[128,16,227]{2,1,0:T(8,128)(2,1)S(1)}, u32[]{:S(2)}, u32[]{:S(2)}) %all-to-all-start) | async-done | bytes 929824 | tf_op jit(solution)/shard_map/all_to_all | solution.py:479
  37.0 0.0 copy-done
  37.0 0.0 copy-done.1
  37.0 0.0 copy-done.2
  37.0 20.6 %encode.1 = (f32[10240,128]{1,0:T(8,128)}, bf16[2048,512]{1,0:T(8,128)(2,1)}) custom-call(s32[2048]{0:T(1024)S(1)} %select_multiply_fusion.target, s32[2048]{0:T(1024)S(1)} %mul.21.halo, bf16[2048,227]{1,0:T(8,128)(2,1)S(1)} %bitcast.16, bf16[2048,512]{1,0:T(8,128)(2,1)} %get-tuple-element.10.mesh_term, f32[10240,128]{1,0:T(8,128)} %get-tuple-element.11.own, ...), custom_call_target="tpu_custom_call" | custom-call | tf_op jit(solution)/shard_map/encode/pallas_call | solution.py:514
  57.7 0.0 copy-start.6
  57.7 5.6 %all-to-all-start.1 = ((bf16[128,16,512]{2,1,0:T(8,128)(2,1)}), bf16[128,16,512]{2,1,0:T(8,128)(2,1)S(1)}, u32[]{:S(2)}, u32[]{:S(2)}) async-start(bf16[128,16,512]{2,1,0:T(8,128)(2,1)} %bitcast.20), calls=%async_computation.1 | async-start | bytes 4194304 | tf_op jit(solution)/shard_map/all_to_all | solution.py:541
  63.3 0.0 copy-done.6
  63.3 21.3 %local_terms.1 = (bf16[2560,512]{1,0:T(8,128)(2,1)}, bf16[4096,512]{1,0:T(8,128)(2,1)}) custom-call(s32[4096]{0:T(1024)S(1)} %broadcast_multiply_fusion.dst, s32[4096]{0:T(1024)S(1)} %get-tuple-element.19.src, f32[10240,128]{1,0:T(8,128)} %get-tuple-element.14.sums_in, bf16[2560,512]{1,0:T(8,128)(2,1)} %mesh.3, bf16[3,512,512]{2,1,0:T(8,128)(2,1)} %node_w.5, ...), custom_call_target="tpu_custom_call" | custom-call | flops 20000000000 | bytes 40000000 | tf_op jit(solution)/shard_map/local_terms/pallas_call | solution.py:546
  84.6 8.4 %all-to-all-done.1 = bf16[128,16,512]{2,1,0:T(8,128)(2,1)S(1)} async-done(((bf16[128,16,512]{2,1,0:T(8,128)(2,1)}), bf16[128,16,512]{2,1,0:T(8,128)(2,1)S(1)}, u32[]{:S(2)}, u32[]{:S(2)}) %all-to-all-start.1) | async-done | bytes 2097184 | tf_op jit(solution)/shard_map/all_to_all | solution.py:541
  92.9 14.6 %edge_update.1 = bf16[4096,512]{1,0:T(8,128)(2,1)} custom-call(s32[4096]{0:T(1024)S(1)} %get-tuple-element.18.src, bf16[2048,512]{1,0:T(8,128)(2,1)S(1)} %bitcast.15, bf16[4,512,512]{2,1,0:T(8,128)(2,1)} %proc_w.3, bf16[4096,512]{1,0:T(8,128)(2,1)} %edges_in.3, bf16[4096,512]{1,0:T(8,128)(2,1)} %get-tuple-element.17.local_in, f32[3,512]{1,0:T(4,128)S(1)} %copy-done.2), custom_call_target="tpu_custom_call" | custom-call | tf_op jit(solution)/shard_map/edge_update/pallas_call | solution.py:578
  (4 shorter events, 0.0 us)
Async XLA Ops:
  0.6 17.8 %copy-start.3 = (s32[1,128,16]{1,2,0:T(8,128)S(1)}, s32[1,128,16]{1,2,0:T(8,128)}, u32[]{:S(2)}) copy-start(s32[1,128,16]{1,2,0:T(8,128)} %param.25) | copy-start | bytes 24580
  0.6 17.9 %copy-start.7 = (s32[1,128]{1,0:T(1,128)S(1)}, s32[1,128]{1,0:T(1,128)}, u32[]{:S(2)}) copy-start(s32[1,128]{1,0:T(1,128)} %param.26) | copy-start | bytes 1540
  0.7 18.1 %copy-start.4 = (s32[1,128,16]{1,2,0:T(8,128)S(1)}, s32[1,128,16]{1,2,0:T(8,128)}, u32[]{:S(2)}) copy-start(s32[1,128,16]{1,2,0:T(8,128)} %param.27) | copy-start | bytes 24580
  0.7 18.3 %copy-start.5 = (s32[4096]{0:T(1024)S(1)}, s32[4096]{0:T(1024)}, u32[]{:S(2)}) copy-start(s32[4096]{0:T(1024)} %param.29) | copy-start | bytes 49156
  6.9 30.1 %all-to-all-start = ((bf16[128,16,227]{2,1,0:T(8,128)(2,1)}), bf16[128,16,227]{2,1,0:T(8,128)(2,1)S(1)}, u32[]{:S(2)}, u32[]{:S(2)}) async-start(bf16[128,16,227]{2,1,0:T(8,128)(2,1)} %bitcast.19), calls=%async_computation | async-start | bytes 2097152 | tf_op jit(solution)/shard_map/all_to_all | solution.py:479
  19.0 18.0 %copy-start = (bf16[512,512]{1,0:T(8,128)(2,1)S(1)}, bf16[512,512]{1,0:T(8,128)(2,1)}, u32[]{:S(2)}) copy-start(bf16[512,512]{1,0:T(8,128)(2,1)} %embed_out.1) | copy-start | bytes 1572868
  19.0 18.0 %copy-start.1 = (bf16[227,512]{1,0:T(8,128)(2,1)S(1)}, bf16[227,512]{1,0:T(8,128)(2,1)}, u32[]{:S(2)}) copy-start(bf16[227,512]{1,0:T(8,128)(2,1)} %embed_in.1) | copy-start | bytes 697348
  19.0 18.0 %copy-start.2 = (f32[3,512]{1,0:T(4,128)S(1)}, f32[3,512]{1,0:T(4,128)}, u32[]{:S(2)}) copy-start(f32[3,512]{1,0:T(4,128)} %gains.5) | copy-start | bytes 18436
  57.7 5.6 %copy-start.6 = (s32[4096]{0:T(1024)S(1)}, s32[4096]{0:T(1024)}, u32[]{:S(2)}) copy-start(s32[4096]{0:T(1024)} %param.28) | copy-start | bytes 49156
  57.7 35.2 %all-to-all-start.1 = ((bf16[128,16,512]{2,1,0:T(8,128)(2,1)}), bf16[128,16,512]{2,1,0:T(8,128)(2,1)S(1)}, u32[]{:S(2)}, u32[]{:S(2)}) async-start(bf16[128,16,512]{2,1,0:T(8,128)(2,1)} %bitcast.20), calls=%async_computation.1 | async-start | bytes 4194304 | tf_op jit(solution)/shard_map/all_to_all | solution.py:541

commit v4 on v3

--- a/solution.py
+++ b/solution.py
@@ -205,7 +205,8 @@
     ]
     for copy in copies:
         copy.start()
-    sums[pl.ds(mesh_rows, 8), :] = jnp.zeros((8, 128), F32)
+    spare = sums.shape[0] - mesh_rows
+    sums[pl.ds(mesh_rows, spare), :] = jnp.zeros((spare, 128), F32)
     for copy in copies[:3]:
         copy.wait()
     step = MESSAGE_STEP
@@ -357,7 +358,7 @@
     w_proc, edges, local, new, senders, first, second, sems, edge_sems,
 ):
     rows = halo.shape[0]
-    step = 512
+    step = 1024
     chunks = rows // step
     edge_step = EDGE_STEP * 2
     edge_chunks = edges.shape[0] // edge_step
@@ -510,7 +511,8 @@
         name="mesh_side",
     )(dst, halo, in_hbm(mesh_latent), in_hbm(enc_w), in_hbm(node_w))
 
-    live = jnp.arange(cap, dtype=jnp.int32)[:, None] < g2m_count
+    slot = jnp.arange(cap, dtype=jnp.int32)[:, None]
+    live = slot < g2m_count
     sums, halo_out = pl.pallas_call(
         encode,
         out_shape=(
@@ -520,7 +522,7 @@
         in_specs=[SMEM, SMEM, VMEM, ANY, ANY, ANY, VMEM, VMEM, ANY, ANY, ANY, VMEM],
         out_specs=(ANY, ANY),
         scratch_shapes=[
-            scratch(mesh_rows * parts + 8),
+            scratch((mesh_rows + cap) * parts),
             scratch(slots, width, BF16),
             scratch(slots * parts),
             scratch(HALO_STEP * parts),
@@ -535,7 +537,7 @@
         compiler_params=params(32),
         name="encode",
     )(
-        jnp.where(live, dst, mesh_rows).T.reshape(-1) * parts, halo.T.reshape(-1) * parts, arrived, in_hbm(mesh_term), in_hbm(own),
+        jnp.where(live, dst, mesh_rows + slot).T.reshape(-1) * parts, halo.T.reshape(-1) * parts, arrived, in_hbm(mesh_term), in_hbm(own),
         in_hbm(own_halo), embed_in, embed_out, in_hbm(enc_w), folded, in_hbm(node_w), gains,
     )
     halo_in = lax.all_to_all(

time: 108 us -> 105 us (0.972)
  Pallas kernels: 76.5 us -> 73 us
    pallas_call x1, Pallas kernels: 20.6 us -> 17.4 us  [shards(): pl.pallas_call(encode, out_shape=(pltpu.HBM((mesh_rows * parts, 128), F32...]
  transfers between devices with their start and end apart: 2 -> 2, of which waited for: 2 -> 2; matrix products, arithmetic and copies ran while one was open for 1% -> 1% of each run, Pallas kernels for 33% -> 34%
where the time goes in v4:
time: 105 us; the launch traced here: 104 us
  Pallas kernels  73 us (70%)
  starting transfers between devices  17.3 us (16%)
  waiting for transfers between devices  12.4 us (12%)
    pallas_call x1, Pallas kernels, shards(): pl.pallas_call(local_terms, out_shape=(pltpu.HBM((mesh_rows, width), BF16...  21.3 us
    pallas_call x1, Pallas kernels, shards(): pl.pallas_call(encode, out_shape=(pltpu.HBM((mesh_rows * parts, 128), F32...  17.4 us
    pallas_call x1, Pallas kernels, shards(): pl.pallas_call(edge_update, out_shape=pltpu.HBM((edges, width), BF16), in...  14.3 us
    pallas_call x1, Pallas kernels, shards(): pl.pallas_call(mesh_side, out_shape=(pltpu.HBM((slots, width), BF16), plt...  13.8 us
    all_to_all x1, starting transfers between devices, shards(): lax.all_to_all(outgoing.reshape(peers, cap, features), axes, split_axis=0...  11.5 us
    all_to_all x1, waiting for transfers between devices, shards(): lax.all_to_all(halo_out.reshape(peers, halo_cap, width), axes, split_axis...  8.36 us
    pallas_call x1, Pallas kernels, shards(): pl.pallas_call(pick_grid, out_shape=pltpu.HBM((slots, features), BF16), i...  6.2 us
    all_to_all x1, starting transfers between devices, shards(): lax.all_to_all(halo_out.reshape(peers, halo_cap, width), axes, split_axis...  5.79 us
  transfers between devices with their start and end apart: 2, of which 2 were waited for; matrix products, arithmetic and copies ran while one was open for 1% of the time, Pallas kernels for 34%

profile of v4, /device:TPU:1, one launch (start us, length us, event | category | flops | bytes accessed | tf_op | source)
XLA Modules:
  0.0 104.4 jit_solution(9395206928027698810)
XLA Ops:
  0.6 0.0 copy-start.3
  0.6 0.0 copy-start.7
  0.7 0.0 copy-start.4
  0.7 0.0 copy-start.5
  0.7 6.2 %pick_grid.1 = bf16[2048,227]{1,0:T(8,128)(2,1)} custom-call(s32[16,128]{1,0:T(8,128)} %bitcast.22, bf16[227,4096]{1,0:T(8,128)(2,1)} %bitcast.21), custom_call_target="tpu_custom_call" | custom-call | tf_op jit(solution)/shard_map/pick_grid/pallas_call | solution.py:461
  6.9 11.5 %all-to-all-start = ((bf16[128,16,227]{2,1,0:T(8,128)(2,1)}), bf16[128,16,227]{2,1,0:T(8,128)(2,1)S(1)}, u32[]{:S(2)}, u32[]{:S(2)}) async-start(bf16[128,16,227]{2,1,0:T(8,128)(2,1)} %bitcast.19), calls=%async_computation | async-start | bytes 2097152 | tf_op jit(solution)/shard_map/all_to_all | solution.py:480
  18.4 0.1 broadcast_in_dim.18
  18.5 0.0 copy-done.3
  18.5 0.1 copy.17
  18.6 0.1 squeeze.11
  18.7 0.0 copy-done.7
  18.7 0.1 iota_compare_fusion
  18.8 0.1 lt.24
  18.9 0.0 copy-done.4
  18.9 0.1 copy.18
  19.0 0.1 mul.21.halo
  19.1 0.0 copy-done.5
  19.1 0.0 copy-start
  19.1 0.0 copy-start.1
  19.1 0.0 copy-start.2
  19.2 13.8 %mesh_side.1 = (bf16[2048,512]{1,0:T(8,128)(2,1)}, f32[10240,128]{1,0:T(8,128)}, bf16[2048,512]{1,0:T(8,128)(2,1)}, bf16[512,512]{1,0:T(8,128)(2,1)S(1)}) custom-call(s32[16,128]{1,0:T(8,128)S(1)} %bitcast.17, s32[16,128]{1,0:T(8,128)S(1)} %bitcast.18, bf16[2560,512]{1,0:T(8,128)(2,1)} %mesh.3, bf16[3,512,512]{2,1,0:T(8,128)(2,1)} %enc_w.3, ...), custom_call_target="tpu_custom_call" | custom-call | flops 10000000000 | bytes 20000000 | tf_op jit(solution)/shard_map/mesh_side/pallas_call | solution.py:486
  33.0 4.1 %all-to-all-done = bf16[128,16,227]{2,1,0:T(8,128)(2,1)S(1)} async-done(((bf16[128,16,227]{2,1,0:T(8,128)(2,1)}), bf16[128,16,227]{2,1,0:T(8,128)(2,1)S(1)}, u32[]{:S(2)}, u32[]{:S(2)}) %all-to-all-start) | async-done | bytes 929824 | tf_op jit(solution)/shard_map/all_to_all | solution.py:480
  37.0 0.0 copy-done
  37.0 0.0 copy-done.1
  37.0 0.0 copy-done.2
  37.0 17.4 %encode.1 = (f32[10240,128]{1,0:T(8,128)}, bf16[2048,512]{1,0:T(8,128)(2,1)}) custom-call(s32[2048]{0:T(1024)S(1)} %select_multiply_fusion.target, s32[2048]{0:T(1024)S(1)} %mul.21.halo, bf16[2048,227]{1,0:T(8,128)(2,1)S(1)} %bitcast.16, bf16[2048,512]{1,0:T(8,128)(2,1)} %get-tuple-element.10.mesh_term, f32[10240,128]{1,0:T(8,128)} %get-tuple-element.11.own, ...), custom_call_target="tpu_custom_call" | custom-call | tf_op jit(solution)/shard_map/encode/pallas_call | solution.py:516
  54.5 0.0 copy-start.6
  54.5 5.8 %all-to-all-start.1 = ((bf16[128,16,512]{2,1,0:T(8,128)(2,1)}), bf16[128,16,512]{2,1,0:T(8,128)(2,1)S(1)}, u32[]{:S(2)}, u32[]{:S(2)}) async-start(bf16[128,16,512]{2,1,0:T(8,128)(2,1)} %bitcast.20), calls=%async_computation.1 | async-start | bytes 4194304 | tf_op jit(solution)/shard_map/all_to_all | solution.py:543
  60.3 0.0 copy-done.6
  60.3 21.3 %local_terms.1 = (bf16[2560,512]{1,0:T(8,128)(2,1)}, bf16[4096,512]{1,0:T(8,128)(2,1)}) custom-call(s32[4096]{0:T(1024)S(1)} %broadcast_multiply_fusion.dst, s32[4096]{0:T(1024)S(1)} %get-tuple-element.19.src, f32[10240,128]{1,0:T(8,128)} %get-tuple-element.14.sums_in, bf16[2560,512]{1,0:T(8,128)(2,1)} %mesh.3, bf16[3,512,512]{2,1,0:T(8,128)(2,1)} %node_w.5, ...), custom_call_target="tpu_custom_call" | custom-call | flops 20000000000 | bytes 40000000 | tf_op jit(solution)/shard_map/local_terms/pallas_call | solution.py:548
  81.6 8.4 %all-to-all-done.1 = bf16[128,16,512]{2,1,0:T(8,128)(2,1)S(1)} async-done(((bf16[128,16,512]{2,1,0:T(8,128)(2,1)}), bf16[128,16,512]{2,1,0:T(8,128)(2,1)S(1)}, u32[]{:S(2)}, u32[]{:S(2)}) %all-to-all-start.1) | async-done | bytes 2097184 | tf_op jit(solution)/shard_map/all_to_all | solution.py:543
  89.9 14.3 %edge_update.1 = bf16[4096,512]{1,0:T(8,128)(2,1)} custom-call(s32[4096]{0:T(1024)S(1)} %get-tuple-element.18.src, bf16[2048,512]{1,0:T(8,128)(2,1)S(1)} %bitcast.15, bf16[4,512,512]{2,1,0:T(8,128)(2,1)} %proc_w.3, bf16[4096,512]{1,0:T(8,128)(2,1)} %edges_in.3, bf16[4096,512]{1,0:T(8,128)(2,1)} %get-tuple-element.17.local_in, f32[3,512]{1,0:T(4,128)S(1)} %copy-done.2), custom_call_target="tpu_custom_call" | custom-call | tf_op jit(solution)/shard_map/edge_update/pallas_call | solution.py:580
  (6 shorter events, 0.0 us)
Async XLA Ops:
  0.6 17.9 %copy-start.3 = (s32[1,128,16]{1,2,0:T(8,128)S(1)}, s32[1,128,16]{1,2,0:T(8,128)}, u32[]{:S(2)}) copy-start(s32[1,128,16]{1,2,0:T(8,128)} %param.25) | copy-start | bytes 24580
  0.6 18.0 %copy-start.7 = (s32[1,128]{1,0:T(1,128)S(1)}, s32[1,128]{1,0:T(1,128)}, u32[]{:S(2)}) copy-start(s32[1,128]{1,0:T(1,128)} %param.26) | copy-start | bytes 1540
  0.7 18.2 %copy-start.4 = (s32[1,128,16]{1,2,0:T(8,128)S(1)}, s32[1,128,16]{1,2,0:T(8,128)}, u32[]{:S(2)}) copy-start(s32[1,128,16]{1,2,0:T(8,128)} %param.27) | copy-start | bytes 24580
  0.7 18.4 %copy-start.5 = (s32[4096]{0:T(1024)S(1)}, s32[4096]{0:T(1024)}, u32[]{:S(2)}) copy-start(s32[4096]{0:T(1024)} %param.29) | copy-start | bytes 49156
  6.9 30.1 %all-to-all-start = ((bf16[128,16,227]{2,1,0:T(8,128)(2,1)}), bf16[128,16,227]{2,1,0:T(8,128)(2,1)S(1)}, u32[]{:S(2)}, u32[]{:S(2)}) async-start(bf16[128,16,227]{2,1,0:T(8,128)(2,1)} %bitcast.19), calls=%async_computation | async-start | bytes 2097152 | tf_op jit(solution)/shard_map/all_to_all | solution.py:480
  19.1 17.9 %copy-start = (bf16[512,512]{1,0:T(8,128)(2,1)S(1)}, bf16[512,512]{1,0:T(8,128)(2,1)}, u32[]{:S(2)}) copy-start(bf16[512,512]{1,0:T(8,128)(2,1)} %embed_out.1) | copy-start | bytes 1572868
  19.1 17.9 %copy-start.1 = (bf16[227,512]{1,0:T(8,128)(2,1)S(1)}, bf16[227,512]{1,0:T(8,128)(2,1)}, u32[]{:S(2)}) copy-start(bf16[227,512]{1,0:T(8,128)(2,1)} %embed_in.1) | copy-start | bytes 697348
  19.1 17.9 %copy-start.2 = (f32[3,512]{1,0:T(4,128)S(1)}, f32[3,512]{1,0:T(4,128)}, u32[]{:S(2)}) copy-start(f32[3,512]{1,0:T(4,128)} %gains.5) | copy-start | bytes 18436
  54.5 5.8 %copy-start.6 = (s32[4096]{0:T(1024)S(1)}, s32[4096]{0:T(1024)}, u32[]{:S(2)}) copy-start(s32[4096]{0:T(1024)} %param.28) | copy-start | bytes 49156
  54.5 35.4 %all-to-all-start.1 = ((bf16[128,16,512]{2,1,0:T(8,128)(2,1)}), bf16[128,16,512]{2,1,0:T(8,128)(2,1)S(1)}, u32[]{:S(2)}, u32[]{:S(2)}) async-start(bf16[128,16,512]{2,1,0:T(8,128)(2,1)} %bitcast.20), calls=%async_computation.1 | async-start | bytes 4194304 | tf_op jit(solution)/shard_map/all_to_all | solution.py:543

commit v5 on v4

--- a/solution.py
+++ b/solution.py
@@ -11,9 +11,9 @@
 SMEM = pl.BlockSpec(memory_space=pltpu.SMEM)
 ANY = pl.BlockSpec(memory_space=pl.ANY)
 STEP = 256
-MESSAGE_STEP = 1024
+MESSAGE_STEP = 2048
 HALO_STEP = 512
-EDGE_STEP = 512
+EDGE_STEP = 1024
 
 
 def params(mebibytes):
@@ -33,9 +33,12 @@
     return half + half * jnp.tanh(half)
 
 
-def norm(value, gain):
-    mean = jnp.mean(value, axis=-1, keepdims=True)
-    centred = value - mean
+def centre(weight):
+    value = weight.astype(F32)
+    return (value - jnp.mean(value, axis=-1, keepdims=True)).astype(BF16)
+
+
+def norm(centred, gain):
     variance = jnp.mean(centred * centred, axis=-1, keepdims=True)
     return centred * lax.rsqrt(variance + 1e-05) * gain
 
@@ -121,8 +124,8 @@
 
 
 def mesh_side(
-    dst, halo, mesh, enc_w, node_w,
-    term_out, own_out, halo_out, folded_out,
+    dst, halo, mesh, enc_w, node_w, embed_out,
+    term_out, own_out, halo_out, folded_out, embed_centred, node_centred,
     table, copies, picked, picked_too, own, terms, halves, latents, w_enc, w_node, sems,
 ):
     rows = mesh.shape[0]
@@ -131,7 +134,7 @@
     chunks = rows // step
     weights = [
         pltpu.make_async_copy(enc_w.at[pl.ds(1, 2)], w_enc, sems.at[0]),
-        pltpu.make_async_copy(node_w.at[pl.ds(0, 2)], w_node, sems.at[1]),
+        pltpu.make_async_copy(node_w, w_node, sems.at[1]),
     ]
     for copy in weights:
         copy.start()
@@ -158,6 +161,8 @@
     outs = [pltpu.make_async_copy(own, own_out, sems.at[0])]
     outs[0].start()
     folded_out[...] = dot(w_enc[1], w_node[1]).astype(BF16)
+    embed_centred[...] = centre(embed_out[...])
+    node_centred[...] = centre(w_node[2])
     step = 64
     parts = 4
     span = slots // parts
@@ -188,7 +193,7 @@
 
 
 def encode(
-    target, halo, rows_in, mesh_term, own, own_halo, embed_in, embed_out, enc_w, folded, node_w,
+    target, halo, rows_in, mesh_term, own, own_halo, embed_in, embed_out, enc_w, folded, node_centred,
     gains, sums_out, halo_out,
     sums, terms, sent, first, second, halves, w_grid, w_message, w_out, halo_rows, sems,
 ):
@@ -200,7 +205,7 @@
         pltpu.make_async_copy(folded, w_message, sems.at[1]),
         pltpu.make_async_copy(mesh_term, terms, sems.at[2]),
         pltpu.make_async_copy(own, sums.at[pl.ds(0, mesh_rows)], sems.at[3]),
-        pltpu.make_async_copy(node_w.at[2], w_out, sems.at[4]),
+        pltpu.make_async_copy(node_centred, w_out, sems.at[4]),
         pltpu.make_async_copy(own_halo, halves, sems.at[5]),
     ]
     for copy in copies:
@@ -266,7 +271,7 @@
 
 
 def local_terms(
-    dst, src, sums_in, mesh, node_w, proc_w, gains, edges_in, mesh_out, out,
+    dst, src, sums_in, mesh, node_centred, proc_w, gains, edges_in, mesh_out, out, proc_centred,
     sums, latents, edges, new, local, w_node, w_proc, receivers, senders, picked, sems, edge_sems,
 ):
     rows = mesh.shape[0]
@@ -274,8 +279,8 @@
     chunks = rows // step
     edge_chunks = edges.shape[0] // step
     weights = [
-        pltpu.make_async_copy(node_w.at[2], w_node, sems.at[0]),
-        pltpu.make_async_copy(proc_w.at[pl.ds(0, 3)], w_proc, sems.at[1]),
+        pltpu.make_async_copy(node_centred, w_node, sems.at[0]),
+        pltpu.make_async_copy(proc_w, w_proc, sems.at[1]),
     ]
 
     def sums_copy(part):
@@ -313,6 +318,7 @@
     senders[pl.ds(rows * 4, 8), :] = jnp.zeros((8, 128), F32)
     for copy in weights:
         copy.wait()
+    proc_centred[...] = centre(w_proc[3])
 
     @pl.loop(0, chunks)
     def _(block):
@@ -354,7 +360,7 @@
 
 
 def edge_update(
-    src, halo, proc_w, edges_in, local_in, gains, out,
+    src, halo, proc_w, proc_centred, edges_in, local_in, gains, out,
     w_proc, edges, local, new, senders, first, second, sems, edge_sems,
 ):
     rows = halo.shape[0]
@@ -363,7 +369,8 @@
     edge_step = EDGE_STEP * 2
     edge_chunks = edges.shape[0] // edge_step
     last = src.shape[0] // EDGE_STEP - 1
-    weights = pltpu.make_async_copy(proc_w.at[pl.ds(2, 2)], w_proc, sems.at[0])
+    weights = pltpu.make_async_copy(proc_w.at[2], w_proc.at[0], sems.at[0])
+    last_weight = pltpu.make_async_copy(proc_centred, w_proc.at[1], sems.at[1])
 
     def edge_copy(part):
         return pltpu.make_async_copy(
@@ -381,6 +388,7 @@
         )
 
     weights.start()
+    last_weight.start()
     for part in range(edge_chunks):
         local_copy(part).start()
         edge_copy(part).start()
@@ -402,6 +410,7 @@
         change = norm(dot(hidden, w_proc[1]), gains[2:3, :])
         new[here, :] = (edges[here, :].astype(F32) + change).astype(BF16)
 
+    last_weight.wait()
     pick(0, first)
 
     @pl.loop(0, edge_chunks)
@@ -483,16 +492,18 @@
 
     dst = g2m_dst[0].T
     halo = halo_rows[0].T
-    mesh_term, own, own_halo, folded = pl.pallas_call(
+    mesh_term, own, own_halo, folded, embed_centred, node_centred = pl.pallas_call(
         mesh_side,
         out_shape=(
             pltpu.HBM((slots, width), BF16),
             pltpu.HBM((mesh_rows * parts, 128), F32),
             pltpu.HBM((halo_slots, width), BF16),
             full(width, width, BF16),
+            full(width, width, BF16),
+            full(width, width, BF16),
         ),
-        in_specs=[SMEM, SMEM, ANY, ANY, ANY],
-        out_specs=(ANY, ANY, ANY, VMEM),
+        in_specs=[SMEM, SMEM, ANY, ANY, ANY, VMEM],
+        out_specs=(ANY, ANY, ANY, VMEM, VMEM, VMEM),
         scratch_shapes=[
             scratch(mesh_rows * parts),
             scratch(mesh_rows * parts),
@@ -503,13 +514,13 @@
             scratch(halo_slots, width, BF16),
             scratch(mesh_rows, width, BF16),
             pltpu.VMEM((2, width, width), BF16),
-            pltpu.VMEM((2, width, width), BF16),
+            pltpu.VMEM((3, width, width), BF16),
             sems(2 + mesh_rows // 512),
         ],
         compiler_params=params(40),
         cost_estimate=cost(10**10, 2 * 10**7),
         name="mesh_side",
-    )(dst, halo, in_hbm(mesh_latent), in_hbm(enc_w), in_hbm(node_w))
+    )(dst, halo, in_hbm(mesh_latent), in_hbm(enc_w), in_hbm(node_w), embed_out)
 
     slot = jnp.arange(cap, dtype=jnp.int32)[:, None]
     live = slot < g2m_count
@@ -538,18 +549,22 @@
         name="encode",
     )(
         jnp.where(live, dst, mesh_rows + slot).T.reshape(-1) * parts, halo.T.reshape(-1) * parts, arrived, in_hbm(mesh_term), in_hbm(own),
-        in_hbm(own_halo), embed_in, embed_out, in_hbm(enc_w), folded, in_hbm(node_w), gains,
+        in_hbm(own_halo), embed_in, embed_centred, in_hbm(enc_w), folded, node_centred, gains,
     )
     halo_in = lax.all_to_all(
         halo_out.reshape(peers, halo_cap, width), axes, split_axis=0, concat_axis=0, tiled=True
     ).reshape(halo_slots, width)
 
     remote = proc_src >= mesh_rows
-    mesh_new, local = pl.pallas_call(
+    mesh_new, local, proc_centred = pl.pallas_call(
         local_terms,
-        out_shape=(pltpu.HBM((mesh_rows, width), BF16), pltpu.HBM((edges, width), BF16)),
+        out_shape=(
+            pltpu.HBM((mesh_rows, width), BF16),
+            pltpu.HBM((edges, width), BF16),
+            pltpu.HBM((width, width), BF16),
+        ),
         in_specs=[SMEM, SMEM, ANY, ANY, ANY, ANY, VMEM, ANY],
-        out_specs=(ANY, ANY),
+        out_specs=(ANY, ANY, VMEM),
         scratch_shapes=[
             scratch(mesh_rows * parts),
             scratch(mesh_rows, width, BF16),
@@ -557,7 +572,7 @@
             scratch(mesh_rows, width, BF16),
             scratch(edges, width, BF16),
             scratch(width, width, BF16),
-            pltpu.VMEM((3, width, width), BF16),
+            pltpu.VMEM((4, width, width), BF16),
             scratch(mesh_rows * parts),
             scratch(mesh_rows * parts + 8),
             scratch(512 * parts),
@@ -572,7 +587,7 @@
         jnp.where(remote, mesh_rows, proc_src) * parts,
         in_hbm(sums),
         in_hbm(mesh_latent),
-        in_hbm(node_w),
+        node_centred,
         in_hbm(proc_w),
         gains,
         in_hbm(edge_latent),
@@ -580,7 +595,7 @@
     edge_new = pl.pallas_call(
         edge_update,
         out_shape=pltpu.HBM((edges, width), BF16),
-        in_specs=[SMEM, VMEM, ANY, ANY, ANY, VMEM],
+        in_specs=[SMEM, VMEM, ANY, ANY, ANY, ANY, VMEM],
         out_specs=ANY,
         scratch_shapes=[
             pltpu.VMEM((2, width, width), BF16),
@@ -590,7 +605,7 @@
             scratch(halo_slots * parts + 8),
             scratch(EDGE_STEP * parts),
             scratch(EDGE_STEP * parts),
-            sems(1),
+            sems(2),
             sems(2, edges // EDGE_STEP // 2),
         ],
         compiler_params=params(28),
@@ -599,6 +614,7 @@
         jnp.where(remote, proc_src - mesh_rows, halo_slots) * parts,
         halo_in,
         in_hbm(proc_w),
+        in_hbm(proc_centred),
         in_hbm(edge_latent),
         in_hbm(local),
         gains,

time: 105 us -> 102 us (0.971)
  Pallas kernels: 73 us -> 70.5 us
    pallas_call x1, Pallas kernels: 14.3 us -> 12.8 us  [shards(): pl.pallas_call(edge_update, out_shape=pltpu.HBM((edges, width), BF16), in...]
    pallas_call x1, Pallas kernels: 17.4 us -> 16.4 us  [shards(): pl.pallas_call(encode, out_shape=(pltpu.HBM((mesh_rows * parts, 128), F32...]
where the time goes in v5:
time: 102 us
  Pallas kernels  70.5 us (69%)
  starting transfers between devices  17.5 us (17%)
  waiting for transfers between devices  12.3 us (12%)
    pallas_call x1, Pallas kernels, shards(): pl.pallas_call(local_terms, out_shape=(pltpu.HBM((mesh_rows, width), BF16...  21.1 us
    pallas_call x1, Pallas kernels, shards(): pl.pallas_call(encode, out_shape=(pltpu.HBM((mesh_rows * parts, 128), F32...  16.4 us
    pallas_call x1, Pallas kernels, shards(): pl.pallas_call(mesh_side, out_shape=(pltpu.HBM((slots, width), BF16), plt...  14 us
    pallas_call x1, Pallas kernels, shards(): pl.pallas_call(edge_update, out_shape=pltpu.HBM((edges, width), BF16), in...  12.8 us
    all_to_all x1, starting transfers between devices, shards(): lax.all_to_all(outgoing.reshape(peers, cap, features), axes, split_axis=0...  11.5 us
    all_to_all x1, waiting for transfers between devices, shards(): lax.all_to_all(halo_out.reshape(peers, halo_cap, width), axes, split_axis...  8.46 us
    pallas_call x1, Pallas kernels, shards(): pl.pallas_call(pick_grid, out_shape=pltpu.HBM((slots, features), BF16), i...  6.25 us
    all_to_all x1, starting transfers between devices, shards(): lax.all_to_all(halo_out.reshape(peers, halo_cap, width), axes, split_axis...  5.95 us
  transfers between devices with their start and end apart: 2, of which 2 were waited for; matrix products, arithmetic and copies ran while one was open for 1% of the time, Pallas kernels for 34%

profile of v5, /device:TPU:1, one launch (start us, length us, event | category | flops | bytes accessed | tf_op | source)
XLA Modules:
  0.0 102.0 jit_solution(3255596173404427235)
XLA Ops:
  0.6 0.0 copy-start.2
  0.6 0.0 copy-start.7
  0.7 0.0 copy-start.3
  0.7 0.0 copy-start.5
  0.7 0.0 copy-start.4
  0.7 6.3 %pick_grid.1 = bf16[2048,227]{1,0:T(8,128)(2,1)} custom-call(s32[16,128]{1,0:T(8,128)} %bitcast.22, bf16[227,4096]{1,0:T(8,128)(2,1)} %bitcast.21), custom_call_target="tpu_custom_call" | custom-call | tf_op jit(solution)/shard_map/pick_grid/pallas_call | solution.py:470
  6.9 11.5 %all-to-all-start = ((bf16[128,16,227]{2,1,0:T(8,128)(2,1)}), bf16[128,16,227]{2,1,0:T(8,128)(2,1)S(1)}, u32[]{:S(2)}, u32[]{:S(2)}) async-start(bf16[128,16,227]{2,1,0:T(8,128)(2,1)} %bitcast.19), calls=%async_computation | async-start | bytes 2097152 | tf_op jit(solution)/shard_map/all_to_all | solution.py:489
  18.5 0.1 broadcast_in_dim.18
  18.6 0.0 copy-done.2
  18.6 0.1 copy.17
  18.7 0.1 squeeze.11
  18.7 0.0 copy-done.7
  18.8 0.1 iota_compare_fusion
  18.8 0.1 lt.24
  18.9 0.0 copy-done.3
  19.0 0.1 copy.18
  19.1 0.1 mul.21.halo
  19.1 0.0 copy-done.5
  19.2 0.0 copy-done.4
  19.2 0.0 copy-start
  19.2 0.0 copy-start.1
  19.2 14.0 %mesh_side.1 = (bf16[2048,512]{1,0:T(8,128)(2,1)}, f32[10240,128]{1,0:T(8,128)}, bf16[2048,512]{1,0:T(8,128)(2,1)}, bf16[512,512]{1,0:T(8,128)(2,1)S(1)}, bf16[5...) custom-call(s32[16,128]{1,0:T(8,128)S(1)} %bitcast.17, s32[16,128]{1,0:T(8,128)S(1)} %bitcast.18, ...), custom_call_target="tpu_custom_call" | custom-call | flops 10000000000 | bytes 20000000 | tf_op jit(solution)/shard_map/mesh_side/pallas_call | solution.py:495
  33.2 3.9 %all-to-all-done = bf16[128,16,227]{2,1,0:T(8,128)(2,1)S(1)} async-done(((bf16[128,16,227]{2,1,0:T(8,128)(2,1)}), bf16[128,16,227]{2,1,0:T(8,128)(2,1)S(1)}, u32[]{:S(2)}, u32[]{:S(2)}) %all-to-all-start) | async-done | bytes 929824 | tf_op jit(solution)/shard_map/all_to_all | solution.py:489
  37.1 0.0 copy-done
  37.1 0.0 copy-done.1
  37.1 16.4 %encode.1 = (f32[10240,128]{1,0:T(8,128)}, bf16[2048,512]{1,0:T(8,128)(2,1)}) custom-call(s32[2048]{0:T(1024)S(1)} %select_multiply_fusion.target, s32[2048]{0:T(1024)S(1)} %mul.21.halo, bf16[2048,227]{1,0:T(8,128)(2,1)S(1)} %bitcast.16, bf16[2048,512]{1,0:T(8,128)(2,1)} %get-tuple-element.13.mesh_term, f32[10240,128]{1,0:T(8,128)} %get-tuple-element.14.own, ...), custom_call_target="tpu_custom_call" | custom-call | tf_op jit(solution)/shard_map/encode/pallas_call | solution.py:527
  53.4 0.0 copy-start.6
  53.5 6.0 %all-to-all-start.1 = ((bf16[128,16,512]{2,1,0:T(8,128)(2,1)}), bf16[128,16,512]{2,1,0:T(8,128)(2,1)S(1)}, u32[]{:S(2)}, u32[]{:S(2)}) async-start(bf16[128,16,512]{2,1,0:T(8,128)(2,1)} %bitcast.20), calls=%async_computation.1 | async-start | bytes 4194304 | tf_op jit(solution)/shard_map/all_to_all | solution.py:554
  59.4 0.0 copy-done.6
  59.4 21.1 %local_terms.1 = (bf16[2560,512]{1,0:T(8,128)(2,1)}, bf16[4096,512]{1,0:T(8,128)(2,1)}, bf16[512,512]{1,0:T(8,128)(2,1)}) custom-call(s32[4096]{0:T(1024)S(1)} %broadcast_multiply_fusion.dst, s32[4096]{0:T(1024)S(1)} %get-tuple-element.25.src, f32[10240,128]{1,0:T(8,128)} %get-tuple-element.19.sums_in, bf16[2560,512]{1,0:T(8,128)(2,1)} %mesh.3, ...), custom_call_target="tpu_custom_call" | custom-call | flops 20000000000 | bytes 40000000 | tf_op jit(solution)/shard_map/local_terms/pallas_call | solution.py:559
  80.6 8.5 %all-to-all-done.1 = bf16[128,16,512]{2,1,0:T(8,128)(2,1)S(1)} async-done(((bf16[128,16,512]{2,1,0:T(8,128)(2,1)}), bf16[128,16,512]{2,1,0:T(8,128)(2,1)S(1)}, u32[]{:S(2)}, u32[]{:S(2)}) %all-to-all-start.1) | async-done | bytes 2097184 | tf_op jit(solution)/shard_map/all_to_all | solution.py:554
  89.1 12.8 %edge_update.1 = bf16[4096,512]{1,0:T(8,128)(2,1)} custom-call(s32[4096]{0:T(1024)S(1)} %get-tuple-element.24.src, bf16[2048,512]{1,0:T(8,128)(2,1)S(1)} %bitcast.15, bf16[4,512,512]{2,1,0:T(8,128)(2,1)} %proc_w.3, bf16[512,512]{1,0:T(8,128)(2,1)} %get-tuple-element.22.proc_centred, bf16[4096,512]{1,0:T(8,128)(2,1)} %edges_in.3, ...), custom_call_target="tpu_custom_call" | custom-call | tf_op jit(solution)/shard_map/edge_update/pallas_call | solution.py:595
  (6 shorter events, 0.0 us)
Async XLA Ops:
  0.6 17.9 %copy-start.2 = (s32[1,128,16]{1,2,0:T(8,128)S(1)}, s32[1,128,16]{1,2,0:T(8,128)}, u32[]{:S(2)}) copy-start(s32[1,128,16]{1,2,0:T(8,128)} %param.25) | copy-start | bytes 24580
  0.6 18.1 %copy-start.7 = (s32[1,128]{1,0:T(1,128)S(1)}, s32[1,128]{1,0:T(1,128)}, u32[]{:S(2)}) copy-start(s32[1,128]{1,0:T(1,128)} %param.26) | copy-start | bytes 1540
  0.7 18.3 %copy-start.3 = (s32[1,128,16]{1,2,0:T(8,128)S(1)}, s32[1,128,16]{1,2,0:T(8,128)}, u32[]{:S(2)}) copy-start(s32[1,128,16]{1,2,0:T(8,128)} %param.27) | copy-start | bytes 24580
  0.7 18.5 %copy-start.5 = (s32[4096]{0:T(1024)S(1)}, s32[4096]{0:T(1024)}, u32[]{:S(2)}) copy-start(s32[4096]{0:T(1024)} %param.29) | copy-start | bytes 49156
  0.7 18.5 %copy-start.4 = (bf16[512,512]{1,0:T(8,128)(2,1)S(1)}, bf16[512,512]{1,0:T(8,128)(2,1)}, u32[]{:S(2)}) copy-start(bf16[512,512]{1,0:T(8,128)(2,1)} %embed_out.1) | copy-start | bytes 1572868
  6.9 30.1 %all-to-all-start = ((bf16[128,16,227]{2,1,0:T(8,128)(2,1)}), bf16[128,16,227]{2,1,0:T(8,128)(2,1)S(1)}, u32[]{:S(2)}, u32[]{:S(2)}) async-start(bf16[128,16,227]{2,1,0:T(8,128)(2,1)} %bitcast.19), calls=%async_computation | async-start | bytes 2097152 | tf_op jit(solution)/shard_map/all_to_all | solution.py:489
  19.2 17.9 %copy-start = (bf16[227,512]{1,0:T(8,128)(2,1)S(1)}, bf16[227,512]{1,0:T(8,128)(2,1)}, u32[]{:S(2)}) copy-start(bf16[227,512]{1,0:T(8,128)(2,1)} %embed_in.1) | copy-start | bytes 697348
  19.2 17.9 %copy-start.1 = (f32[3,512]{1,0:T(4,128)S(1)}, f32[3,512]{1,0:T(4,128)}, u32[]{:S(2)}) copy-start(f32[3,512]{1,0:T(4,128)} %gains.5) | copy-start | bytes 18436
  53.4 6.0 %copy-start.6 = (s32[4096]{0:T(1024)S(1)}, s32[4096]{0:T(1024)}, u32[]{:S(2)}) copy-start(s32[4096]{0:T(1024)} %param.28) | copy-start | bytes 49156
  53.5 35.6 %all-to-all-start.1 = ((bf16[128,16,512]{2,1,0:T(8,128)(2,1)}), bf16[128,16,512]{2,1,0:T(8,128)(2,1)S(1)}, u32[]{:S(2)}, u32[]{:S(2)}) async-start(bf16[128,16,512]{2,1,0:T(8,128)(2,1)} %bitcast.20), calls=%async_computation.1 | async-start | bytes 4194304 | tf_op jit(solution)/shard_map/all_to_all | solution.py:554

commit v6 on v5

--- a/solution.py
+++ b/solution.py
@@ -28,9 +28,12 @@
     return jnp.dot(a, b, preferred_element_type=F32)
 
 
+def silu_of_double(half):
+    return half + half * jnp.tanh(half)
+
+
 def silu(v):
-    half = 0.5 * v
-    return half + half * jnp.tanh(half)
+    return silu_of_double(0.5 * v)
 
 
 def centre(weight):
@@ -155,12 +158,12 @@
         latent_copy(block).wait()
         value = latents[pl.ds(at, step), :]
         put_rows(table, at, dot(value, w_enc[0]))
-        put_rows(own, at, dot(value, w_node[0]))
+        put_rows(own, at, 0.5 * dot(value, w_node[0]))
         put_rows(copies, at, value.astype(F32))
 
     outs = [pltpu.make_async_copy(own, own_out, sems.at[0])]
     outs[0].start()
-    folded_out[...] = dot(w_enc[1], w_node[1]).astype(BF16)
+    folded_out[...] = (0.5 * dot(w_enc[1], w_node[1])).astype(BF16)
     embed_centred[...] = centre(embed_out[...])
     node_centred[...] = centre(w_node[2])
     step = 64
@@ -188,8 +191,8 @@
         copy.wait()
 
 
-def node_update(pre, own, w_out, gain):
-    return (own.astype(F32) + norm(dot(silu(pre).astype(BF16), w_out), gain)).astype(BF16)
+def node_update(half, own, w_out, gain):
+    return (own.astype(F32) + norm(dot(silu_of_double(half).astype(BF16), w_out), gain)).astype(BF16)
 
 
 def encode(
@@ -350,7 +353,7 @@
 
         here = pl.ds(start, step)
         value = dot(edges[here, :], w_proc[0]) + get_rows(picked, 0, step, 4)
-        local[here, :] = value.astype(BF16)
+        local[here, :] = (0.5 * value).astype(BF16)
         local_copy(block).start()
 
     for part in range(chunks):
@@ -398,7 +401,7 @@
     @pl.loop(0, chunks)
     def _(block):
         at = pl.multiple_of(block * step, step)
-        put_rows(senders, at, dot(halo[pl.ds(at, step), :], w_proc[0]))
+        put_rows(senders, at, 0.5 * dot(halo[pl.ds(at, step), :], w_proc[0]))
 
     def pick(block, into):
         at = block * EDGE_STEP
@@ -406,7 +409,7 @@
 
     def update(block, source):
         here = pl.ds(pl.multiple_of(block * EDGE_STEP, EDGE_STEP), EDGE_STEP)
-        hidden = silu(local[here, :].astype(F32) + get_rows(source, 0, EDGE_STEP, 4)).astype(BF16)
+        hidden = silu_of_double(local[here, :].astype(F32) + get_rows(source, 0, EDGE_STEP, 4)).astype(BF16)
         change = norm(dot(hidden, w_proc[1]), gains[2:3, :])
         new[here, :] = (edges[here, :].astype(F32) + change).astype(BF16)
 

time: 102 us -> 102 us (level)
  transfers between devices with their start and end apart: 2 -> 2, of which waited for: 2 -> 2; matrix products, arithmetic and copies ran while one was open for 1% -> 1% of each run, Pallas kernels for 34% -> 35%
where the time goes in v6:
time: 102 us
  Pallas kernels  70.1 us (69%)
  starting transfers between devices  17.5 us (17%)
  waiting for transfers between devices  12.3 us (12%)
    pallas_call x1, Pallas kernels, shards(): pl.pallas_call(local_terms, out_shape=(pltpu.HBM((mesh_rows, width), BF16...  21.2 us
    pallas_call x1, Pallas kernels, shards(): pl.pallas_call(encode, out_shape=(pltpu.HBM((mesh_rows * parts, 128), F32...  16.3 us
    pallas_call x1, Pallas kernels, shards(): pl.pallas_call(mesh_side, out_shape=(pltpu.HBM((slots, width), BF16), plt...  14 us
    pallas_call x1, Pallas kernels, shards(): pl.pallas_call(edge_update, out_shape=pltpu.HBM((edges, width), BF16), in...  12.3 us
    all_to_all x1, starting transfers between devices, shards(): lax.all_to_all(outgoing.reshape(peers, cap, features), axes, split_axis=0...  11.5 us
    all_to_all x1, waiting for transfers between devices, shards(): lax.all_to_all(halo_out.reshape(peers, halo_cap, width), axes, split_axis...  8.44 us
    pallas_call x1, Pallas kernels, shards(): pl.pallas_call(pick_grid, out_shape=pltpu.HBM((slots, features), BF16), i...  6.25 us
    all_to_all x1, starting transfers between devices, shards(): lax.all_to_all(halo_out.reshape(peers, halo_cap, width), axes, split_axis...  5.97 us
  transfers between devices with their start and end apart: 2, of which 2 were waited for; matrix products, arithmetic and copies ran while one was open for 1% of the time, Pallas kernels for 35%

profile of v6, /device:TPU:1, one launch (start us, length us, event | category | flops | bytes accessed | tf_op | source)
XLA Modules:
  0.0 101.5 jit_solution(15511019937215457526)
XLA Ops:
  0.6 0.0 copy-start.2
  0.6 0.0 copy-start.7
  0.7 0.0 copy-start.3
  0.7 0.0 copy-start.5
  0.7 0.0 copy-start.4
  0.7 6.3 %pick_grid.1 = bf16[2048,227]{1,0:T(8,128)(2,1)} custom-call(s32[16,128]{1,0:T(8,128)} %bitcast.22, bf16[227,4096]{1,0:T(8,128)(2,1)} %bitcast.21), custom_call_target="tpu_custom_call" | custom-call | tf_op jit(solution)/shard_map/pick_grid/pallas_call | solution.py:473
  6.9 11.5 %all-to-all-start = ((bf16[128,16,227]{2,1,0:T(8,128)(2,1)}), bf16[128,16,227]{2,1,0:T(8,128)(2,1)S(1)}, u32[]{:S(2)}, u32[]{:S(2)}) async-start(bf16[128,16,227]{2,1,0:T(8,128)(2,1)} %bitcast.19), calls=%async_computation | async-start | bytes 2097152 | tf_op jit(solution)/shard_map/all_to_all | solution.py:492
  18.5 0.1 broadcast_in_dim.18
  18.6 0.0 copy-done.2
  18.6 0.1 copy.17
  18.7 0.1 squeeze.11
  18.7 0.0 copy-done.7
  18.8 0.1 iota_compare_fusion
  18.8 0.1 lt.24
  18.9 0.0 copy-done.3
  19.0 0.1 copy.18
  19.1 0.1 mul.21.halo
  19.1 0.0 copy-done.5
  19.2 0.0 copy-done.4
  19.2 0.0 copy-start
  19.2 0.0 copy-start.1
  19.2 14.0 %mesh_side.1 = (bf16[2048,512]{1,0:T(8,128)(2,1)}, f32[10240,128]{1,0:T(8,128)}, bf16[2048,512]{1,0:T(8,128)(2,1)}, bf16[512,512]{1,0:T(8,128)(2,1)S(1)}, bf16[5...) custom-call(s32[16,128]{1,0:T(8,128)S(1)} %bitcast.17, s32[16,128]{1,0:T(8,128)S(1)} %bitcast.18, ...), custom_call_target="tpu_custom_call" | custom-call | flops 10000000000 | bytes 20000000 | tf_op jit(solution)/shard_map/mesh_side/pallas_call | solution.py:498
  33.2 3.8 %all-to-all-done = bf16[128,16,227]{2,1,0:T(8,128)(2,1)S(1)} async-done(((bf16[128,16,227]{2,1,0:T(8,128)(2,1)}), bf16[128,16,227]{2,1,0:T(8,128)(2,1)S(1)}, u32[]{:S(2)}, u32[]{:S(2)}) %all-to-all-start) | async-done | bytes 929824 | tf_op jit(solution)/shard_map/all_to_all | solution.py:492
  37.1 0.0 copy-done
  37.1 0.0 copy-done.1
  37.1 16.3 %encode.1 = (f32[10240,128]{1,0:T(8,128)}, bf16[2048,512]{1,0:T(8,128)(2,1)}) custom-call(s32[2048]{0:T(1024)S(1)} %select_multiply_fusion.target, s32[2048]{0:T(1024)S(1)} %mul.21.halo, bf16[2048,227]{1,0:T(8,128)(2,1)S(1)} %bitcast.16, bf16[2048,512]{1,0:T(8,128)(2,1)} %get-tuple-element.13.mesh_term, f32[10240,128]{1,0:T(8,128)} %get-tuple-element.14.own, ...), custom_call_target="tpu_custom_call" | custom-call | tf_op jit(solution)/shard_map/encode/pallas_call | solution.py:530
  53.4 0.0 copy-start.6
  53.4 6.0 %all-to-all-start.1 = ((bf16[128,16,512]{2,1,0:T(8,128)(2,1)}), bf16[128,16,512]{2,1,0:T(8,128)(2,1)S(1)}, u32[]{:S(2)}, u32[]{:S(2)}) async-start(bf16[128,16,512]{2,1,0:T(8,128)(2,1)} %bitcast.20), calls=%async_computation.1 | async-start | bytes 4194304 | tf_op jit(solution)/shard_map/all_to_all | solution.py:557
  59.4 0.0 copy-done.6
  59.4 21.2 %local_terms.1 = (bf16[2560,512]{1,0:T(8,128)(2,1)}, bf16[4096,512]{1,0:T(8,128)(2,1)}, bf16[512,512]{1,0:T(8,128)(2,1)}) custom-call(s32[4096]{0:T(1024)S(1)} %broadcast_multiply_fusion.dst, s32[4096]{0:T(1024)S(1)} %get-tuple-element.25.src, f32[10240,128]{1,0:T(8,128)} %get-tuple-element.19.sums_in, bf16[2560,512]{1,0:T(8,128)(2,1)} %mesh.3, ...), custom_call_target="tpu_custom_call" | custom-call | flops 20000000000 | bytes 40000000 | tf_op jit(solution)/shard_map/local_terms/pallas_call | solution.py:562
  80.6 8.4 %all-to-all-done.1 = bf16[128,16,512]{2,1,0:T(8,128)(2,1)S(1)} async-done(((bf16[128,16,512]{2,1,0:T(8,128)(2,1)}), bf16[128,16,512]{2,1,0:T(8,128)(2,1)S(1)}, u32[]{:S(2)}, u32[]{:S(2)}) %all-to-all-start.1) | async-done | bytes 2097184 | tf_op jit(solution)/shard_map/all_to_all | solution.py:557
  89.0 12.3 %edge_update.1 = bf16[4096,512]{1,0:T(8,128)(2,1)} custom-call(s32[4096]{0:T(1024)S(1)} %get-tuple-element.24.src, bf16[2048,512]{1,0:T(8,128)(2,1)S(1)} %bitcast.15, bf16[4,512,512]{2,1,0:T(8,128)(2,1)} %proc_w.3, bf16[512,512]{1,0:T(8,128)(2,1)} %get-tuple-element.22.proc_centred, bf16[4096,512]{1,0:T(8,128)(2,1)} %edges_in.3, ...), custom_call_target="tpu_custom_call" | custom-call | tf_op jit(solution)/shard_map/edge_update/pallas_call | solution.py:598
  (6 shorter events, 0.0 us)
Async XLA Ops:
  0.6 17.9 %copy-start.2 = (s32[1,128,16]{1,2,0:T(8,128)S(1)}, s32[1,128,16]{1,2,0:T(8,128)}, u32[]{:S(2)}) copy-start(s32[1,128,16]{1,2,0:T(8,128)} %param.25) | copy-start | bytes 24580
  0.6 18.1 %copy-start.7 = (s32[1,128]{1,0:T(1,128)S(1)}, s32[1,128]{1,0:T(1,128)}, u32[]{:S(2)}) copy-start(s32[1,128]{1,0:T(1,128)} %param.26) | copy-start | bytes 1540
  0.7 18.3 %copy-start.3 = (s32[1,128,16]{1,2,0:T(8,128)S(1)}, s32[1,128,16]{1,2,0:T(8,128)}, u32[]{:S(2)}) copy-start(s32[1,128,16]{1,2,0:T(8,128)} %param.27) | copy-start | bytes 24580
  0.7 18.5 %copy-start.5 = (s32[4096]{0:T(1024)S(1)}, s32[4096]{0:T(1024)}, u32[]{:S(2)}) copy-start(s32[4096]{0:T(1024)} %param.29) | copy-start | bytes 49156
  0.7 18.5 %copy-start.4 = (bf16[512,512]{1,0:T(8,128)(2,1)S(1)}, bf16[512,512]{1,0:T(8,128)(2,1)}, u32[]{:S(2)}) copy-start(bf16[512,512]{1,0:T(8,128)(2,1)} %embed_out.1) | copy-start | bytes 1572868
  6.9 30.1 %all-to-all-start = ((bf16[128,16,227]{2,1,0:T(8,128)(2,1)}), bf16[128,16,227]{2,1,0:T(8,128)(2,1)S(1)}, u32[]{:S(2)}, u32[]{:S(2)}) async-start(bf16[128,16,227]{2,1,0:T(8,128)(2,1)} %bitcast.19), calls=%async_computation | async-start | bytes 2097152 | tf_op jit(solution)/shard_map/all_to_all | solution.py:492
  19.2 17.9 %copy-start = (bf16[227,512]{1,0:T(8,128)(2,1)S(1)}, bf16[227,512]{1,0:T(8,128)(2,1)}, u32[]{:S(2)}) copy-start(bf16[227,512]{1,0:T(8,128)(2,1)} %embed_in.1) | copy-start | bytes 697348
  19.2 17.9 %copy-start.1 = (f32[3,512]{1,0:T(4,128)S(1)}, f32[3,512]{1,0:T(4,128)}, u32[]{:S(2)}) copy-start(f32[3,512]{1,0:T(4,128)} %gains.5) | copy-start | bytes 18436
  53.4 6.0 %copy-start.6 = (s32[4096]{0:T(1024)S(1)}, s32[4096]{0:T(1024)}, u32[]{:S(2)}) copy-start(s32[4096]{0:T(1024)} %param.28) | copy-start | bytes 49156
  53.4 35.6 %all-to-all-start.1 = ((bf16[128,16,512]{2,1,0:T(8,128)(2,1)}), bf16[128,16,512]{2,1,0:T(8,128)(2,1)S(1)}, u32[]{:S(2)}, u32[]{:S(2)}) async-start(bf16[128,16,512]{2,1,0:T(8,128)(2,1)} %bitcast.20), calls=%async_computation.1 | async-start | bytes 4194304 | tf_op jit(solution)/shard_map/all_to_all | solution.py:557
